TPU v7x, 32 devices: a whole 2x2x4 slice. The times are simulated.
32 devices in a mesh: dp: 8 (over z, y), tensor: 4 (over x, core).
Axes of the slice: x: 2, y: 2, z: 4, core: 2. Of those that a mesh axis runs over, the one named last changes fastest.
Arguments:
- inputs: float32 [16384, 768], P('dp'), may hold values from -6 to 6
- segment_ids: int32 [32, 512], P('dp'), may hold values from 0 to 7, never falling along the last dimension, each value on 1 to 128 neighbouring positions
- w_qkv: float32 [3, 768, 768], P(None, None, 'tensor')
- b_qv: float32 [2, 768], P(None, 'tensor'), may hold values from -3 to 3
- w_out: float32 [768, 768], P('tensor')
- w_ff1: float32 [768, 3072], P(None, 'tensor')
- b_ff1: float32 [3072], P('tensor'), may hold values from -3 to 3
- w_ff2: float32 [3072, 768], P('tensor')
- norm_gains: float32 [2, 768], replicated, may hold values from 0.25 to 1.75
- shift_biases: float32 [4, 768], replicated, may hold values from -2 to 2
- act_ranges: float32 [4], replicated, may hold values from 1 to 24
- cotangent: float32 [16384, 768], P('dp'), may hold values from -6 to 6
Outputs:
- layer_out: float32 [16384, 768], P('dp')
- input_grad: float32 [16384, 768], P('dp')
- grad_qkv: float32 [3, 768, 768], P(None, None, 'tensor')
- grad_bqv: float32 [2, 768], P(None, 'tensor')
- grad_out: float32 [768, 768], P('tensor')
- grad_ff1: float32 [768, 3072], P(None, 'tensor')
- grad_bff1: float32 [3072], P('tensor')
- grad_ff2: float32 [3072, 768], P('tensor')
- grad_gains: float32 [2, 768], P(None, 'tensor')
- grad_shifts: float32 [4, 768], P(None, 'tensor')
- weight_max: float32 [6], replicated
Inputs may be any that keep to these rules, and one draw needn't show every extreme that they name: `segment_ids`: equal ids within a packed row mark one example; ids never fall along a row.
All inputs are finite; a program needn't handle non-finite values.
Results may differ from a plain program's by a relative error of at most 0.019.
Values may be sent and summed in bfloat16 or wider, within the bound.
A program may use at most 192 MiB of HBM per device.

v0:
```python
import math

import jax
import jax.numpy as jnp
from jax import lax
from jax.sharding import PartitionSpec as P

HD = 64


TWO_PI = 2.0 * math.pi
MASKED = -1e30
EPSILON = 1e-06
ROOT_HALF = 0.7071067811865476
INV_ROOT_TWO_PI = 0.3989422804014327


def stair_weight(matrix, largest):
    levels = 127.0 * matrix / largest
    return (largest / 127.0 * (levels - jnp.sin(TWO_PI * levels) / TWO_PI)).astype(jnp.bfloat16)


def stair_act(values, bound):
    squash = jnp.tanh(values / bound)
    levels = 127.0 * squash
    result = bound / 127.0 * (levels - jnp.sin(TWO_PI * levels) / TWO_PI)
    slopes = 1.0 - squash * squash
    return (result.astype(jnp.bfloat16), slopes)


def norm_forward(hidden, gain_row, shift_row):
    average = jnp.mean(hidden, -1, keepdims=True)
    centred = hidden - average
    inverse = lax.rsqrt(jnp.mean(centred * centred, -1, keepdims=True) + EPSILON)
    normed = centred * inverse
    return (normed * gain_row + shift_row, normed, inverse)


def norm_backward(gradient, normed, inverse, gain_row):
    scaled = gradient * gain_row
    return inverse * (
        scaled
        - jnp.mean(scaled, -1, keepdims=True)
        - normed * jnp.mean(scaled * normed, -1, keepdims=True)
    )


def gelu_exact(values):
    return 0.5 * values * (1.0 + lax.erf(values * ROOT_HALF))


def gelu_slope(values):
    return (
        0.5 * (1.0 + lax.erf(values * ROOT_HALF))
        + values * jnp.exp(-0.5 * values * values) * INV_ROOT_TWO_PI
    )


def masked_scores(queries, keys_in, segment):
    scores = (
        jnp.einsum("qhd,khd->hqk", queries, keys_in, preferred_element_type=jnp.float32) * 0.125
    )
    same_doc = segment[:, None] == segment[None, :]
    return jnp.where(same_doc[None], scores, MASKED)


def attend_forward(pieces):
    queries, keys_in, values_in, segment = pieces
    scores = masked_scores(queries, keys_in, segment)
    largest = jnp.max(scores, -1, keepdims=True)
    weights_exp = jnp.exp(scores - largest)
    total = jnp.sum(weights_exp, -1, keepdims=True)
    probs = (weights_exp / total).astype(jnp.bfloat16)
    context = jnp.einsum("hqk,khd->qhd", probs, values_in, preferred_element_type=jnp.float32)
    return (context, largest + jnp.log(total))


def attend_backward(pieces):
    queries, keys_in, values_in, segment, log_total, d_context = pieces
    probs = jnp.exp(masked_scores(queries, keys_in, segment) - log_total)
    d_values = jnp.einsum(
        "hqk,qhd->khd", probs.astype(jnp.bfloat16), d_context, preferred_element_type=jnp.float32
    )
    d_probs = jnp.einsum("qhd,khd->hqk", d_context, values_in, preferred_element_type=jnp.float32)
    d_scores = probs * (d_probs - jnp.sum(probs * d_probs, -1, keepdims=True))
    d_low = d_scores.astype(jnp.bfloat16)
    d_queries = (
        jnp.einsum("hqk,khd->qhd", d_low, keys_in, preferred_element_type=jnp.float32) * 0.125
    )
    d_keys = jnp.einsum("hqk,qhd->khd", d_low, queries, preferred_element_type=jnp.float32) * 0.125
    return (d_queries, d_keys, d_values)


def per_device(
    inputs,
    segment_ids,
    w_qkv,
    b_qv,
    w_out,
    w_ff1,
    b_ff1,
    w_ff2,
    norm_gains,
    shift_biases,
    act_ranges,
    cotangent,
):
    token_count = inputs.shape[0]
    model_width = inputs.shape[1]
    local_cols = w_qkv.shape[2]
    row_count = segment_ids.shape[0]
    row_length = segment_ids.shape[1]
    local_top = jnp.concatenate(
        [
            jnp.max(jnp.abs(w_qkv), axis=(1, 2)),
            jnp.max(jnp.abs(w_out))[None],
            jnp.max(jnp.abs(w_ff1))[None],
            jnp.max(jnp.abs(w_ff2))[None],
        ]
    )
    weight_max = lax.pmax(local_top, "tensor")
    qkv_low = jnp.stack([stair_weight(w_qkv[member], weight_max[member]) for member in range(3)])
    out_low = stair_weight(w_out, weight_max[3])
    ff1_low = stair_weight(w_ff1, weight_max[4])
    ff2_low = stair_weight(w_ff2, weight_max[5])

    def to_heads(matrix):
        return matrix.reshape(row_count, row_length, local_cols // HD, HD)

    x_low, x_slope = stair_act(inputs, act_ranges[0])
    proj = jnp.einsum("td,jde->jte", x_low, qkv_low, preferred_element_type=jnp.float32)
    q_low = (proj[0] + b_qv[0]).astype(jnp.bfloat16)
    k_low = proj[1].astype(jnp.bfloat16)
    v_low = (proj[2] + b_qv[1]).astype(jnp.bfloat16)
    context, log_total = lax.map(
        attend_forward, (to_heads(q_low), to_heads(k_low), to_heads(v_low), segment_ids)
    )
    context = context.reshape(token_count, local_cols)
    c_low, c_slope = stair_act(context, act_ranges[1])
    attn = (
        lax.psum(
            jnp.dot(c_low, out_low, preferred_element_type=jnp.float32).astype(jnp.bfloat16),
            "tensor",
        ).astype(jnp.float32)
        + shift_biases[0]
    )
    first, normed1, inverse1 = norm_forward(inputs + attn, norm_gains[0], shift_biases[1])
    n_low, n_slope = stair_act(first, act_ranges[2])
    pre = jnp.dot(n_low, ff1_low, preferred_element_type=jnp.float32) + b_ff1
    g_low, g_slope = stair_act(gelu_exact(pre), act_ranges[3])
    ffn = (
        lax.psum(
            jnp.dot(g_low, ff2_low, preferred_element_type=jnp.float32).astype(jnp.bfloat16),
            "tensor",
        ).astype(jnp.float32)
        + shift_biases[2]
    )
    layer_out, normed2, inverse2 = norm_forward(first + ffn, norm_gains[1], shift_biases[3])
    d_second = norm_backward(cotangent, normed2, inverse2, norm_gains[1])
    d_ffn_low = d_second.astype(jnp.bfloat16)
    grad_ff2 = jnp.einsum("tf,td->fd", g_low, d_ffn_low, preferred_element_type=jnp.float32)
    d_act = (
        jnp.einsum("td,fd->tf", d_ffn_low, ff2_low, preferred_element_type=jnp.float32) * g_slope
    )
    d_pre = d_act * gelu_slope(pre)
    d_pre_low = d_pre.astype(jnp.bfloat16)
    grad_bff1 = jnp.sum(d_pre, 0)
    grad_ff1 = jnp.einsum("td,tf->df", n_low, d_pre_low, preferred_element_type=jnp.float32)
    d_normed = lax.psum(
        jnp.einsum("tf,df->td", d_pre_low, ff1_low, preferred_element_type=jnp.float32).astype(
            jnp.bfloat16
        ),
        "tensor",
    ).astype(jnp.float32)
    d_first = d_second + d_normed * n_slope
    d_res1 = norm_backward(d_first, normed1, inverse1, norm_gains[0])
    d_attn_low = d_res1.astype(jnp.bfloat16)
    grad_out = jnp.einsum("tc,td->cd", c_low, d_attn_low, preferred_element_type=jnp.float32)
    d_ctx = (
        jnp.einsum("td,cd->tc", d_attn_low, out_low, preferred_element_type=jnp.float32) * c_slope
    )
    d_ctx_low = d_ctx.astype(jnp.bfloat16)
    d_queries, d_keys, d_values = lax.map(
        attend_backward,
        (
            to_heads(q_low),
            to_heads(k_low),
            to_heads(v_low),
            segment_ids,
            log_total,
            to_heads(d_ctx_low),
        ),
    )
    d_proj = jnp.stack(
        [
            d_queries.reshape(token_count, local_cols),
            d_keys.reshape(token_count, local_cols),
            d_values.reshape(token_count, local_cols),
        ]
    ).astype(jnp.bfloat16)
    grad_bqv = jnp.sum(jnp.stack([d_proj[0], d_proj[2]]), axis=1, dtype=jnp.float32)
    grad_qkv = jnp.einsum("td,jte->jde", x_low, d_proj, preferred_element_type=jnp.float32)
    d_x = lax.psum(
        jnp.einsum("jte,jde->td", d_proj, qkv_low, preferred_element_type=jnp.float32).astype(
            jnp.bfloat16
        ),
        "tensor",
    ).astype(jnp.float32)
    input_grad = d_res1 + d_x * x_slope
    share = model_width // lax.axis_size("tensor")
    start = lax.axis_index("tensor") * share
    gains_full = jnp.stack([jnp.sum(d_first * normed1, 0), jnp.sum(cotangent * normed2, 0)])
    shifts_full = jnp.stack(
        [jnp.sum(d_res1, 0), jnp.sum(d_first, 0), jnp.sum(d_second, 0), jnp.sum(cotangent, 0)]
    )
    grad_gains = lax.dynamic_slice_in_dim(gains_full, start, share, 1)
    grad_shifts = lax.dynamic_slice_in_dim(shifts_full, start, share, 1)
    grad_qkv, grad_bqv, grad_out, grad_ff1, grad_bff1, grad_ff2, grad_gains, grad_shifts = lax.psum(
        (grad_qkv, grad_bqv, grad_out, grad_ff1, grad_bff1, grad_ff2, grad_gains, grad_shifts), "dp"
    )
    return (
        layer_out,
        input_grad,
        grad_qkv,
        grad_bqv,
        grad_out,
        grad_ff1,
        grad_bff1,
        grad_ff2,
        grad_gains,
        grad_shifts,
        weight_max,
    )


def solution(mesh):
    return jax.shard_map(
        per_device,
        mesh=mesh,
        in_specs=(
            P("dp", None),
            P("dp", None),
            P(None, None, "tensor"),
            P(None, "tensor"),
            P("tensor", None),
            P(None, "tensor"),
            P("tensor"),
            P("tensor", None),
            P(),
            P(),
            P(),
            P("dp", None),
        ),
        out_specs=(
            P("dp", None),
            P("dp", None),
            P(None, None, "tensor"),
            P(None, "tensor"),
            P("tensor", None),
            P(None, "tensor"),
            P("tensor"),
            P("tensor", None),
            P(None, "tensor"),
            P(None, "tensor"),
            P(),
        ),
        check_vma=False,
    )
```

profile of v0, /device:TPU:0, one launch (start us, length us, event | category | flops | bytes accessed | tf_op | source)
XLA Modules:
  0.0 824.5 jit_solution(10884026350964699957)
XLA Ops:
  7.3 2.6 abs_reduce_fusion
  11.4 2.0 pad_maximum_fusion.3
  13.4 8.3 %pmax.7 = f32[6]{0:T(128)S(1)} all-reduce(f32[6]{0:T(128)S(1)} %pad_maximum_fusion.3), channel_id=1, replica_groups=mesh['dp'=8,'tensor'=4] {'tensor'}, use_global_device_ids=true, to_apply=%region_4.0 | all-reduce | flops 6 | bytes 48 | tf_op jit(solution)/shard_map/pmax | solution.py:121
  25.5 8.1 multiply_convert_fusion.10
  33.7 26.1 %convolution_bitcast_fusion = f32[3,2048,192]{1,2,0:T(8,128)S(1)} fusion(f32[]{:T(128)S(6)} %div.169, f32[2048,768]{1,0:T(8,128)} %param.16, f32[]{:T(128)} %bitcast.26, bf16[1,768,192]{1,2,0:T(8,128)(2,1)S(1)} %get-tuple-element.217, bf16[1,768,192]{1,2,0:T(8,128)(2,1)S(1)} %get-tuple-element.218, bf16[1,768,192]{1,2,0:T(8,128)(2,1)S(1)} %get-tuple-element.216), kind=kOutput, calls=%fused_computation.92 | convolution fusion | flops 1823834112 | bytes 11894792 | tf_op jit(solution)/shard_map/td,jde->jte/dot_general | solution.py:131
  62.7 2.2 squeeze.73
  64.9 3.0 convert_element_type.101
  69.2 2.2 squeeze.72
  71.4 2.9 fusion.55
  74.3 14.2 %while.28 = (s32[]{:T(128)}, f32[4,512,3,64]{1,3,2,0:T(8,128)}, f32[4,3,512,1]{2,1,3,0:T(4,128)S(1)}, bf16[4,512,3,64]{1,3,2,0:T(8,128)(2,1)S(1)}, s32[4,512]{1,...) while((s32[]{:T(128)}, f32[4,512,3,64]{1,3,2,0:T(8,128)}, ...), condition=%wide.region_8.9_spmd.clone, body=%wide.region_5.8_spmd.sunk.clone | while | flops 211024384 | bytes 11536477 | solution.py:135
  76.1 1.8 fusion.136
  79.6 1.8 fusion.136
  83.2 1.8 fusion.136
  86.7 1.8 fusion.136
  88.6 8.1 multiply_subtract_fusion
  98.5 5.2 convolution_convert_fusion.2
  106.4 9.9 %multiply_convert_fusion.16.clone.5 = bf16[768,768]{1,0:T(8,128)(2,1)S(1)} fusion(f32[768,768]{1,0:T(8,128)} %param.21, f32[]{:T(128)} %bitcast.32, f32[]{:T(128)S(6)} %div.187), kind=kLoop, calls=%fused_computation.99.clone.1.clone.clone.clone.2 | loop fusion | flops 4128768 | bytes 3538952 | tf_op jit(solution)/shard_map/convert_element_type | solution.py:28
  116.3 56.4 %all-reduce.8.cloned.1.call-done = bf16[2048,768]{1,0:T(8,128)(2,1)} async-done(((bf16[2048,768]{1,0:T(8,128)(2,1)}), bf16[2048,768]{1,0:T(8,128)(2,1)}) %all-reduce.8.cloned.1.call-update) | async-done | bytes 3145744 | tf_op jit(solution)/shard_map/psum | solution.py:141
  172.7 4.6 fusion.84
  178.2 1.8 copy-done
  179.9 49.8 %multiply_convert_fusion.1 = (bf16[2048,768]{1,0:T(8,128)(2,1)S(1)}, f32[2048,768]{1,0:T(8,128)}) fusion(f32[]{:T(128)} %bitcast.30, f32[768]{0:T(1024)S(1)} %copy-done.46, f32[]{:T(128)S(6)} %div.182, f32[]{:T(128)S(6)} %div.183, f32[]{:T(128)} %bitcast.31, f32[768]{0:T(1024)S(1)} %get-tuple-element.151, f32[768]{0:T(1024)S(1)} %get-tuple-element.155, ...), kind=kOutput, calls=%fused_computation.76 | convolution fusion | flops 2452094976 | bytes 16933904 | tf_op jit(solution)/shard_map/dot_general | solution.py:149
  231.4 14.1 %convolution_convert_fusion.1 = bf16[2048,768]{1,0:T(8,128)(2,1)} fusion(bf16[2048,768]{1,0:T(8,128)(2,1)S(1)} %get-tuple-element.234, f32[768,768]{1,0:T(8,128)S(1)} %copy-done.24, f32[]{:T(128)} %bitcast.33, f32[]{:T(128)S(6)} %div.194), kind=kOutput, calls=%fused_computation.91 | convolution fusion | flops 2421620736 | bytes 8650760 | tf_op jit(solution)/shard_map/dot_general | solution.py:153
  247.7 2.6 copy.44
  250.3 1.7 copy.55
  252.0 62.2 %all-reduce.10.cloned.1.call-done = bf16[2048,768]{1,0:T(8,128)(2,1)} async-done(((bf16[2048,768]{1,0:T(8,128)(2,1)}), bf16[2048,768]{1,0:T(8,128)(2,1)}) %all-reduce.10.cloned.1.call-update) | async-done | bytes 3145744 | tf_op jit(solution)/shard_map/psum | solution.py:152
  314.2 5.0 fusion.83
  320.1 2.7 multiply_reduce_fusion.1
  322.9 4.9 fusion.81
  327.8 4.1 fusion.63
  332.0 17.4 %fusion.89 = (f32[768]{0:T(1024)}, bf16[2048,768]{1,0:T(8,128)(2,1)S(1)}) fusion(f32[]{:T(128)} %bitcast.30, f32[2048,768]{1,0:T(8,128)} %get-tuple-element.235, f32[768]{0:T(1024)S(1)} %copy-done.47, f32[768,768]{1,0:T(8,128)S(1)} %copy-done.25, f32[]{:T(128)} %bitcast.33, f32[]{:T(128)S(6)} %div.194, f32[2048,768]{1,0:T(8,128)S(1)} %get-tuple-element.201), kind=kOutput, calls=%fused_computation.174 | convolution fusion | flops 2449931520 | bytes 18094092 | tf_op jit(solution)/shard_map/td,fd->tf/dot_general | solution.py:163
  351.0 14.3 %convolution_convert_fusion = bf16[2048,768]{1,0:T(8,128)(2,1)} fusion(bf16[2048,768]{1,0:T(8,128)(2,1)S(1)} %get-tuple-element.237, f32[768,768]{1,0:T(8,128)S(1)} %copy-done.8, f32[]{:T(128)} %bitcast.32, f32[]{:T(128)S(6)} %div.187), kind=kOutput, calls=%fused_computation.90 | convolution fusion | flops 2421620736 | bytes 8650760 | tf_op jit(solution)/shard_map/tf,df->td/dot_general | solution.py:170
  365.4 31.0 %fusion.60 = f32[768,768]{1,0:T(8,128)} fusion(bf16[2048,768]{1,0:T(8,128)(2,1)} %copy-done.48, f32[]{:T(128)S(6)} %div.183, f32[2048,768]{1,0:T(8,128)} %copy-done, f32[]{:T(128)} %bitcast.31, f32[768]{0:T(1024)S(1)} %get-tuple-element.151, f32[768]{0:T(1024)S(1)} %get-tuple-element.155, f32[2048]{0:T(1024)S(1)} %add_rsqrt_fusion.1, ...), kind=kOutput, calls=%fused_computation.113 | convolution fusion | flops 2433220608 | bytes 11819016 | tf_op jit(solution)/shard_map/td,tf->df/dot_general | solution.py:168
  396.4 37.7 %all-reduce.12.cloned.1.call-done = bf16[2048,768]{1,0:T(8,128)(2,1)} async-done(((bf16[2048,768]{1,0:T(8,128)(2,1)}), bf16[2048,768]{1,0:T(8,128)(2,1)}) %all-reduce.12.cloned.1.call-update) | async-done | bytes 3145744 | tf_op jit(solution)/shard_map/psum | solution.py:169
  434.1 9.7 %multiply_reduce_fusion.2 = (f32[768]{0:T(1024)}, f32[2048]{0:T(1024)S(1)}, f32[2048]{0:T(1024)S(1)}, f32[768]{0:T(1024)S(1)}, f32[2048,768]{1,0:T(8,128)S(1)}) fusion(f32[2048,768]{1,0:T(8,128)} %copy-done, f32[2048]{0:T(1024)S(1)} %add_rsqrt_fusion.1, f32[2048]{0:T(1024)S(1)} %broadcast_multiply_fusion.5, f32[768]{0:T(1024)S(1)} %get-tuple-element.155, ...), kind=kLoop, calls=%fused_computation.66 | loop fusion | flops 26733056 | bytes 22065156 | tf_op jit(solution)/shard_map/reduce_sum | solution.py:212
  443.8 4.7 fusion.82
  448.5 2.7 copy-done.1
  451.2 5.2 fusion.54
  456.4 3.1 reshape.184
  459.5 2.2 copy.46
  461.6 29.4 %while.29 = (s32[]{:T(128)}, bf16[4,512,3,64]{1,3,2,0:T(8,128)(2,1)S(1)}, bf16[4,512,3,64]{1,3,2,0:T(8,128)(2,1)}, bf16[4,512,3,64]{1,3,2,0:T(8,128)(2,1)}, bf16...) while((s32[]{:T(128)}, ...), condition=%wide.region_22.23_spmd.clone, body=%wide.region_20.22_spmd.sunk.clone | while | flops 510851584 | bytes 39300324 | solution.py:183
  491.0 1.8 copy.49
  497.5 4.1 bitcast_convert_fusion
  502.8 4.5 fusion.57
  507.3 27.0 %convolution_bitcast_fusion.1 = f32[3,768,192]{1,2,0:T(8,128)} fusion(bf16[3,2048,192]{1,2,0:T(8,128)(2,1)S(1)} %copy-done.36, f32[]{:T(128)S(6)} %div.169, f32[2048,768]{1,0:T(8,128)} %param.16, f32[]{:T(128)} %bitcast.26), kind=kOutput, calls=%fused_computation.120 | convolution fusion | flops 1822949376 | bytes 10420232 | tf_op jit(solution)/shard_map/td,jte->jde/dot_general | solution.py:202
  535.4 37.1 %all-reduce = (f32[2,192]{1,0:T(2,128)}, f32[768]{0:T(1024)}, f32[2,192]{1,0:T(2,128)}, f32[4,192]{1,0:T(4,128)}) all-reduce(f32[2,192]{1,0:T(2,128)S(1)} %convert_reduce_fusion, f32[768]{0:T(1024)S(1)} %copy-done.44, f32[2,192]{1,0:T(2,128)S(1)} %fusion.71, f32[4,192]{1,0:T(4,128)S(1)} %fusion.70), channel_id=1, replica_groups=mesh['dp'=8,'tensor'=4] {'dp'}, use_global_device_ids=true, to_apply=%region_26.27 | all-reduce | flops 2304 | bytes 18432 | tf_op jit(solution)/shard_map/psum | solution.py:218
  572.6 9.6 %multiply_add_fusion = f32[2048,768]{1,0:T(8,128)} fusion(f32[2048,768]{1,0:T(8,128)} %copy-done.1, bf16[2048,768]{1,0:T(8,128)(2,1)} %all-reduce.14.cloned.1.call-done, f32[2048,768]{1,0:T(8,128)} %param.16, f32[]{:T(128)} %bitcast.26), kind=kLoop, calls=%fused_computation.67 | loop fusion | flops 9437184 | bytes 22020100 | tf_op jit(solution)/shard_map/add | solution.py:209
  582.2 229.0 %all-reduce.16.cloned.1.call-done = (f32[3,768,192]{1,2,0:T(8,128)}, f32[192,768]{1,0:T(8,128)}, f32[768,768]{1,0:T(8,128)}, f32[768,768]{1,0:T(8,128)}) async-done(((f32[3,768,192]{1,2,0:T(8,128)}, f32[192,768]{1,0:T(8,128)}, f32[768,768]{1,0:T(8,128)}, f32[768,768]{1,0:T(8,128)}), (f32[3,768,192]{1,2,0:T(8,128)}, f32[192,768]{1,0:T(8,128)}, f32[768,768]{1,0:T(8,128)}, ...) | async-done | bytes 7077904 | tf_op jit(solution)/shard_map/psum | solution.py:218
  811.2 2.9 copy.98
  (242 shorter events, 61.0 us)
Async XLA Ops:
  7.2 2.7 copy-start.7
  7.2 3.4 copy-start.22
  7.2 165.5 %all-reduce.8.cloned.1.call-start = ((), (), s32[]{:S(2)}) async-start(), calls=%async_computation | async-start | bytes 6291456 | tf_op jit(solution)/shard_map/psum | solution.py:141
  7.3 4.0 copy-start.9
  7.3 14.5 %copy-start.42 = (f32[4]{0:T(128)S(1)}, f32[4]{0:T(128)}, u32[]{:S(2)}) copy-start(f32[4]{0:T(128)} %param.26) | copy-start | bytes 52
  10.6 14.9 %copy-start.10 = (f32[3,768,192]{1,2,0:T(8,128)S(1)}, f32[3,768,192]{1,2,0:T(8,128)}, u32[]{:S(2)}) copy-start(f32[3,768,192]{1,2,0:T(8,128)} %param.18) | copy-start | bytes 5308420
  21.8 38.1 %copy-start.38 = (f32[6]{0:T(128)}, f32[6]{0:T(128)S(1)}, u32[]{:S(2)}) copy-start(f32[6]{0:T(128)S(1)} %pmax.7) | copy-start | bytes 76
  33.6 26.2 %copy-start.29 = (bf16[1,768,192]{1,2,0:T(8,128)(2,1)}, bf16[1,768,192]{1,2,0:T(8,128)(2,1)S(1)}, u32[]{:S(2)}) copy-start(bf16[1,768,192]{1,2,0:T(8,128)(2,1)S(1)} %get-tuple-element.216) | copy-start | bytes 884740
  33.7 26.2 %copy-start.31 = (bf16[1,768,192]{1,2,0:T(8,128)(2,1)}, bf16[1,768,192]{1,2,0:T(8,128)(2,1)S(1)}, u32[]{:S(2)}) copy-start(bf16[1,768,192]{1,2,0:T(8,128)(2,1)S(1)} %get-tuple-element.217) | copy-start | bytes 884740
  33.7 26.2 %copy-start.33 = (bf16[1,768,192]{1,2,0:T(8,128)(2,1)}, bf16[1,768,192]{1,2,0:T(8,128)(2,1)S(1)}, u32[]{:S(2)}) copy-start(bf16[1,768,192]{1,2,0:T(8,128)(2,1)S(1)} %get-tuple-element.218) | copy-start | bytes 884740
  71.4 2.9 copy-start.37
  88.6 9.0 %copy-start.3 = (bf16[4,512,3,64]{1,3,2,0:T(8,128)(2,1)}, bf16[4,512,3,64]{1,3,2,0:T(8,128)(2,1)S(1)}, u32[]{:S(2)}) copy-start(bf16[4,512,3,64]{1,3,2,0:T(8,128)(2,1)S(1)} %get-tuple-element.471) | copy-start | bytes 2359300
  88.6 9.0 %copy-start.12 = (bf16[4,512,3,64]{1,3,2,0:T(8,128)(2,1)}, bf16[4,512,3,64]{1,3,2,0:T(8,128)(2,1)S(1)}, u32[]{:S(2)}) copy-start(bf16[4,512,3,64]{1,3,2,0:T(8,128)(2,1)S(1)} %get-tuple-element.474) | copy-start | bytes 2359300
  88.6 9.9 %copy-start.23 = (f32[192,768]{1,0:T(8,128)S(1)}, f32[192,768]{1,0:T(8,128)}, u32[]{:S(2)}) copy-start(f32[192,768]{1,0:T(8,128)} %param.20) | copy-start | bytes 1769476
  98.5 7.8 copy-start.43
  98.5 7.8 copy-start.41
  103.7 210.5 %all-reduce.10.cloned.1.call-start = ((), (), s32[]{:S(2)}) async-start(), calls=%async_computation.1 | async-start | bytes 6291456 | tf_op jit(solution)/shard_map/psum | solution.py:152
  177.3 2.7 copy-start
  177.3 2.6 copy-start.46
  179.9 51.5 %copy-start.24 = (f32[768,768]{1,0:T(8,128)S(1)}, f32[768,768]{1,0:T(8,128)}, u32[]{:S(2)}) copy-start(f32[768,768]{1,0:T(8,128)} %param.23) | copy-start | bytes 7077892
  229.8 1.7 copy-start.20
  245.5 188.6 %all-reduce.12.cloned.1.call-start = ((), (), s32[]{:S(2)}) async-start(), calls=%async_computation.2 | async-start | bytes 6291456 | tf_op jit(solution)/shard_map/psum | solution.py:169
  245.9 1.8 copy-start.5
  247.7 72.4 %slice-start = ((s8[6291456]{0:T(1024)(128)(4,1)}), s8[2097152]{0:T(1024)(128)(4,1)S(1)}, s32[]{:S(2)}) async-start(s8[6291456]{0:T(1024)(128)(4,1)} %bitcast.183), calls=%async_computation.5 | async-start | bytes 4194304
  314.2 5.9 slice-start.1
  322.9 4.9 copy-start.21
  327.8 4.2 copy-start.2
  327.8 4.2 copy-start.25
  327.8 4.2 copy-start.47
  332.0 19.1 %copy-start.8 = (f32[768,768]{1,0:T(8,128)S(1)}, f32[768,768]{1,0:T(8,128)}, u32[]{:S(2)}) copy-start(f32[768,768]{1,0:T(8,128)} %param.21) | copy-start | bytes 7077892
  349.4 1.7 copy-start.48
  365.4 207.2 %all-reduce.14.cloned.1.call-start = ((), (), s32[]{:S(2)}) async-start(), calls=%async_computation.3 | async-start | bytes 6291456 | tf_op jit(solution)/shard_map/psum | solution.py:203
  443.8 7.4 copy-start.11
  448.5 2.7 copy-start.1
  456.4 5.3 copy-start.4
  456.4 5.3 copy-start.6
  466.0 1.6 copy-start.17
  473.3 1.6 copy-start.17
  487.9 1.6 copy-start.17
  491.0 3.6 copy-start.19
  495.3 2.3 copy-start.30
  495.9 1.7 copy-start.32
  495.9 1.7 copy-start.34
  501.7 309.5 %all-reduce.16.cloned.1.call-start = ((), (), s32[]{:S(2)}) async-start(), calls=%async_computation.4 | async-start | bytes 14155776 | tf_op jit(solution)/shard_map/psum | solution.py:218
  502.8 4.5 copy-start.36
  811.2 3.0 copy-start.28
  811.2 3.8 copy-start.27
  814.1 2.2 copy-start.26
  (20 other events, 20.8 us)
Sparse Core Ops, SparseCore 0:
  103.9 68.7 all-reduce.7
  245.6 68.5 all-reduce.9
  365.5 68.5 all-reduce.11
  501.8 68.5 all-reduce.13
  575.2 235.9 all-reduce.15
where the time goes:
time: 835 us; the launch traced here: 825 us
  waiting for transfers between devices  385 us (46%)
  matrix products  235 us (28%)
  other arithmetic  86.7 us (10%)
  local copies, waits for them, and re-layouts  50.4 us (6%)
  blocking collectives  45.4 us (5%)
  between operations  20.9 us (3%)
    psum x1, waiting for transfers between devices, per_device(): lax.psum((grad_qkv, grad_bqv, grad_out, grad_ff1, grad_bff1, grad_ff2, gr...  229 us
    psum x1, waiting for transfers between devices, per_device(): lax.psum(jnp.dot(g_low, ff2_low, preferred_element_type=jnp.float32).asty...  62.2 us
    psum x1, waiting for transfers between devices, per_device(): lax.psum(jnp.dot(c_low, out_low, preferred_element_type=jnp.float32).asty...  56.4 us
    dot_general x1, matrix products, per_device(): pre = jnp.dot(n_low, ff1_low, preferred_element_type=jnp.float32) + b_ff1  49.8 us
    psum x1, waiting for transfers between devices, per_device(): lax.psum(jnp.einsum('tf,df->td', d_pre_low, ff1_low, preferred_element_ty...  37.7 us
    psum x1, blocking collectives, per_device(): lax.psum((grad_qkv, grad_bqv, grad_out, grad_ff1, grad_bff1, grad_ff2, gr...  37.1 us
    dot_general x1, matrix products, per_device(): jnp.einsum('td,tf->df', n_low, d_pre_low, preferred_element_type=jnp.floa...  31 us
    dot_general x1, matrix products, per_device(): jnp.einsum('td,jte->jde', x_low, d_proj, preferred_element_type=jnp.float32)  27 us
  transfers between devices with their start and end apart: 5, of which 4 were waited for; matrix products, arithmetic and copies ran while one was open for 11% of the time, Pallas kernels for 0%

commit v1 on v0

v1 whole, which is shorter than its diff:
```python
import functools
import math

import jax
import jax.numpy as jnp
from jax import lax
from jax.experimental import pallas as pl
from jax.experimental.pallas import tpu as pltpu
from jax.sharding import PartitionSpec as P

HD = 64
SPAN = 128
QB = 256
MASKED = -1e30
EPSILON = 1e-06
ROOT_HALF = 0.7071067811865476
INV_ROOT_TWO_PI = 0.3989422804014327
STAIR = (
    6.579734980213376,
    -12.987641368031495,
    12.20087719668052,
    -6.61489684889321,
    2.04264519055443,
)
MIB = 1 << 20
MESH = pl.DeviceIdType.MESH
F32 = jnp.float32
BF16 = jnp.bfloat16
ANY = pl.BlockSpec(memory_space=pl.ANY)
VMEM = pl.BlockSpec(memory_space=pltpu.VMEM)
SMEM = pl.BlockSpec(memory_space=pltpu.SMEM)
S = jax.ShapeDtypeStruct


def flip(value, bit):
    return value + bit - 2 * bit * ((value // bit) % 2)


def dot_nn(left, right):
    return lax.dot_general(left, right, (((1,), (0,)), ((), ())), preferred_element_type=F32)


def dot_nt(left, right):
    return lax.dot_general(left, right, (((1,), (1,)), ((), ())), preferred_element_type=F32)


def dot_tn(left, right):
    return lax.dot_general(left, right, (((0,), (0,)), ((), ())), preferred_element_type=F32)


def stairs(levels):
    whole = jnp.round(levels)
    rest = levels - whole
    square = rest * rest
    curve = STAIR[4]
    for factor in STAIR[3::-1]:
        curve = curve * square + factor
    return whole + rest * square * curve


def quantize(values, bound):
    squash = jnp.tanh(values * (1.0 / bound))
    return stairs(127.0 * squash) * (bound / 127.0), squash


def norm(hidden):
    centred = hidden - jnp.mean(hidden, -1, keepdims=True)
    inverse = lax.rsqrt(jnp.mean(centred * centred, -1, keepdims=True) + EPSILON)
    return centred * inverse, inverse


def norm_back(scaled, normed, inverse):
    return inverse * (
        scaled
        - jnp.mean(scaled, -1, keepdims=True)
        - normed * jnp.mean(scaled * normed, -1, keepdims=True)
    )


def windows(length):
    found = []
    for first in range(0, length, QB):
        low = max(0, first - SPAN)
        found.append((first, low, min(length, first + QB + SPAN) - low))
    return found


def gather_kernel(
    wqkv, wout, wff1, wff2, bqv, bff1,
    wt_all, wo_all, w1_all, w2_all, small_out,
    f_qkv, f_out, f_1, f_2, q_qkv, q_out, q_1, q_2, small,
    load_sem, local_sem, small_send, small_recv,
    sib_send, sib_recv, far_send, far_recv, side_send, side_recv, pass_send, pass_recv,
):
    t, d = lax.axis_index("tensor"), lax.axis_index("dp")
    y = d % 2
    sib, far, side = (d, flip(t, 1)), (d, flip(t, 2)), (flip(d, 1), t)
    loads = [
        pltpu.make_async_copy(src, dst, load_sem.at[i])
        for i, (src, dst) in enumerate(((wqkv, f_qkv), (wout, f_out), (wff1, f_1), (wff2, f_2)))
    ]
    for load in loads:
        load.start()
    peers = [sib, far, (d, flip(flip(t, 1), 2))]
    barrier = pltpu.get_barrier_semaphore()
    for peer in peers + [side]:
        pl.semaphore_signal(barrier, inc=1, device_id=peer, device_id_type=MESH)
    pl.semaphore_wait(barrier, 4)

    cols = f_qkv.shape[2]
    width = f_out.shape[1]
    for load in loads:
        load.wait()
    tops = [jnp.max(jnp.abs(f_qkv[j]), axis=(0, 1), keepdims=True) for j in range(3)]
    tops += [jnp.max(jnp.abs(f[...]), axis=(0, 1), keepdims=True) for f in (f_out, f_1, f_2)]
    zeros = jnp.zeros((8, width), F32)
    small[pl.ds(t, 1)] = zeros[None]
    small[pl.ds(t, 1), 0:1, :] = bff1[...][None]
    small[pl.ds(t, 1), 1:3, 0:cols] = bqv[...][None]
    row = jnp.concatenate([jnp.broadcast_to(top, (1, 128)) for top in tops], axis=1)
    small[pl.ds(t, 1), 3:4, :] = row[None]
    sends = []
    for i, peer in enumerate(peers):
        copy = pltpu.make_async_remote_copy(
            src_ref=small.at[t], dst_ref=small.at[t], send_sem=small_send.at[i],
            recv_sem=small_recv.at[i], device_id=peer, device_id_type=MESH,
        )
        copy.start()
        sends.append(copy)
    for copy in sends:
        copy.wait()
    top_row = jnp.max(small[:, 3:4, :], axis=0)
    small_out[...] = small[...]

    def weight(value, j):
        top = top_row[:, 128 * j : 128 * j + 1]
        return (stairs(value * (127.0 / top)) * (top / 127.0)).astype(BF16)

    def slot(full, i, s, half):
        if i == 0:
            part = cols // 2
            if half is None:
                return full.at[:, pl.ds(pl.multiple_of(s * cols, 16), cols)]
            return full.at[:, pl.ds(pl.multiple_of(s * cols + half * part, 16), part)]
        if i == 1:
            part = cols // 2
            if half is None:
                return full.at[pl.ds(pl.multiple_of(s * cols, 16), cols)]
            return full.at[pl.ds(pl.multiple_of(s * cols + half * part, 16), part)]
        if half is None:
            return full.at[s]
        part = full.shape[1] // 2
        return full.at[s, pl.ds(pl.multiple_of(half * part, 16), part)]

    def own_half(own, i, half):
        if i == 0:
            part = cols // 2
            return own.at[:, pl.ds(pl.multiple_of(half * part, 16), part)]
        part = own.shape[0] // 2
        return own.at[pl.ds(pl.multiple_of(half * part, 16), part)]

    fulls = (wt_all, wo_all, w1_all, w2_all)
    owns = (q_qkv, q_out, q_1, q_2)
    pending = []
    for i in range(4):
        if i == 0:
            for j in range(3):
                q_qkv[j] = jnp.transpose(
                    (stairs(f_qkv[j] * (127.0 / top_row[:, 128 * j : 128 * j + 1]))
                     * (top_row[:, 128 * j : 128 * j + 1] / 127.0))
                ).astype(BF16)
        elif i == 1:
            q_out[...] = weight(f_out[...], 3)
        elif i == 2:
            q_1[...] = weight(f_1[...], 4)
        else:
            q_2[...] = weight(f_2[...], 5)
        far_copy = pltpu.make_async_remote_copy(
            src_ref=own_half(owns[i], i, y), dst_ref=slot(fulls[i], i, t, y),
            send_sem=far_send.at[i], recv_sem=far_recv.at[i], device_id=far, device_id_type=MESH,
        )
        far_copy.start()
        sib_copy = pltpu.make_async_remote_copy(
            src_ref=owns[i], dst_ref=slot(fulls[i], i, t, None),
            send_sem=sib_send.at[i], recv_sem=sib_recv.at[i], device_id=sib, device_id_type=MESH,
        )
        sib_copy.start()
        local = pltpu.make_async_copy(owns[i], slot(fulls[i], i, t, None), local_sem.at[i])
        local.start()
        pending.append((far_copy, sib_copy, local))
    passed = []
    for i in range(4):
        far_copy, sib_copy, local = pending[i]
        far_copy.wait_recv()
        there = slot(fulls[i], i, flip(t, 2), y)
        side_copy = pltpu.make_async_remote_copy(
            src_ref=there, dst_ref=there, send_sem=side_send.at[i], recv_sem=side_recv.at[i],
            device_id=side, device_id_type=MESH,
        )
        side_copy.start()
        one = pltpu.make_async_remote_copy(
            src_ref=there, dst_ref=there, send_sem=pass_send.at[i], recv_sem=pass_recv.at[i],
            device_id=sib, device_id_type=MESH,
        )
        one.start()
        passed.append((side_copy, one))
    for i in range(4):
        side_copy, one = passed[i]
        side_copy.wait_recv()
        there = slot(fulls[i], i, flip(t, 2), 1 - y)
        two = pltpu.make_async_remote_copy(
            src_ref=there, dst_ref=there, send_sem=pass_send.at[4 + i],
            recv_sem=pass_recv.at[4 + i], device_id=sib, device_id_type=MESH,
        )
        two.start()
        passed[i] = (side_copy, one, two)
    for i in range(4):
        far_copy, sib_copy, local = pending[i]
        side_copy, one, two = passed[i]
        far_copy.wait_send()
        sib_copy.wait()
        local.wait()
        side_copy.wait_send()
        one.wait()
        two.wait()


def gather_weights(w_qkv, w_out, w_ff1, w_ff2, b_qv, b_ff1):
    _, width, cols = w_qkv.shape
    shards = 4
    hidden = w_ff1.shape[1]
    dma = pltpu.SemaphoreType.DMA
    return pl.pallas_call(
        gather_kernel,
        out_shape=(
            S((3, shards * cols, width), BF16),
            S((shards * cols, width), BF16),
            S((shards, width, hidden), BF16),
            S((shards, hidden, width), BF16),
            S((shards, 8, width), F32),
        ),
        in_specs=[ANY] * 4 + [VMEM] * 2,
        out_specs=(ANY,) * 4 + (VMEM,),
        scratch_shapes=[
            pltpu.VMEM((3, width, cols), F32),
            pltpu.VMEM((cols, width), F32),
            pltpu.VMEM((width, hidden), F32),
            pltpu.VMEM((hidden, width), F32),
            pltpu.VMEM((3, cols, width), BF16),
            pltpu.VMEM((cols, width), BF16),
            pltpu.VMEM((width, hidden), BF16),
            pltpu.VMEM((hidden, width), BF16),
            pltpu.VMEM((shards, 8, width), F32),
            dma((4,)), dma((4,)), dma((3,)), dma((3,)),
            dma((4,)), dma((4,)), dma((4,)), dma((4,)), dma((4,)), dma((4,)), dma((8,)), dma((8,)),
        ],
        compiler_params=pltpu.CompilerParams(
            collective_id=1, has_side_effects=True, vmem_limit_bytes=56 * MIB
        ),
        name="gather_weights",
    )(w_qkv, w_out, w_ff1, w_ff2, b_qv, b_ff1.reshape(1, -1))


def attend_kernel(
    place, x_ref, seg_ref, wt_ref, wo_ref, small_ref, gains, shifts, ranges,
    xq_ref, q_ref, k_ref, v_ref, p_ref, cq_ref, cs_ref, nq_ref, xh_ref, inv_ref,
    bias,
):
    length, width = x_ref.shape
    wins = windows(length)
    x = x_ref[...]
    xq = quantize(x, ranges[0])[0].astype(BF16)
    xq_ref[...] = xq
    cols = width // 4

    def both(row):
        parts = [small_ref[s, row : row + 1, 0:cols] for s in range(4)]
        return jnp.concatenate(parts, axis=1)

    q_ref[...] = (dot_nt(xq, wt_ref[0]) + both(1)).astype(BF16)
    k_ref[...] = dot_nt(xq, wt_ref[1]).astype(BF16)
    v_ref[...] = (dot_nt(xq, wt_ref[2]) + both(2)).astype(BF16)
    seg = seg_ref[0].astype(F32)
    seg_col = jnp.transpose(jnp.broadcast_to(seg, (128, length)))
    for b, (first, low, size) in enumerate(wins):
        for lane in range(0, size, 128):
            same = seg_col[first : first + QB] == seg[:, low + lane : low + lane + 128]
            bias[b, :, lane : lane + 128] = jnp.where(same, 0.0, MASKED)
    lanes = lax.broadcasted_iota(jnp.int32, (QB, 128), 1) < HD

    def pair(p, _):
        at = pl.ds(pl.multiple_of(p * 128, 128), 128)
        for b, (first, low, size) in enumerate(wins):
            queries = q_ref[first : first + QB, at].astype(F32) * 0.125
            keys = k_ref[low : low + size, at]
            values = v_ref[low : low + size, at]
            results = []
            for head in range(2):
                mine = lanes if head == 0 else jnp.logical_not(lanes)
                chosen = jnp.where(mine, queries, 0.0).astype(BF16)
                scores = dot_nt(chosen, keys) + bias[b]
                weights = jnp.exp(scores - jnp.max(scores, -1, keepdims=True))
                total = jnp.sum(weights, -1, keepdims=True)
                probs = (weights * (1.0 / total)).astype(BF16)
                p_ref[2 * p + head, first : first + QB, 0:size] = probs
                results.append(dot_nn(probs, values))
            context = jnp.where(lanes, results[0], results[1])
            coded, squash = quantize(context, ranges[1])
            cq_ref[first : first + QB, at] = coded.astype(BF16)
            cs_ref[first : first + QB, at] = (1.0 - squash * squash).astype(BF16)
        return 0

    lax.fori_loop(0, width // 128, pair, 0)
    attn = dot_nn(cq_ref[...], wo_ref[...]) + shifts[0:1]
    normed, inverse = norm(x_ref[...] + attn)
    xh_ref[...] = normed
    inv_ref[...] = jnp.broadcast_to(inverse, (length, 128))
    first_norm = normed * gains[0:1] + shifts[1:2]
    nq_ref[...] = quantize(first_norm, ranges[2])[0].astype(BF16)


def attend(place, inputs, segment_ids, wt, wo, small, gains, shifts, ranges):
    rows, length = segment_ids.shape
    tokens, width = inputs.shape
    mine = rows // 2
    half = tokens // 2
    size = max(w[2] for w in windows(length))
    by_row = lambda r, place: (r, 0)
    whole = lambda n: (lambda r, place: (0,) * n)
    return pl.pallas_call(
        attend_kernel,
        out_shape=(
            S((half, width), BF16),
            S((half, width), BF16),
            S((half, width), BF16),
            S((half, width), BF16),
            S((mine * (width // HD), length, size), BF16),
            S((half, width), BF16),
            S((half, width), BF16),
            S((half, width), BF16),
            S((half, width), F32),
            S((half, 128), F32),
        ),
        grid_spec=pltpu.PrefetchScalarGridSpec(
            num_scalar_prefetch=1,
            grid=(mine,),
            in_specs=[
                pl.BlockSpec((length, width), lambda r, place: (place[0] * mine + r, 0)),
                pl.BlockSpec((1, 1, length), lambda r, place: (place[0] * mine + r, 0, 0)),
                pl.BlockSpec(wt.shape, whole(3)),
                pl.BlockSpec(wo.shape, whole(2)),
                pl.BlockSpec(small.shape, whole(3)),
                pl.BlockSpec(gains.shape, whole(2)),
                pl.BlockSpec(shifts.shape, whole(2)),
                SMEM,
            ],
            out_specs=(
                pl.BlockSpec((length, width), by_row),
                pl.BlockSpec((length, width), by_row),
                pl.BlockSpec((length, width), by_row),
                pl.BlockSpec((length, width), by_row),
                pl.BlockSpec((width // HD, length, size), lambda r, place: (r, 0, 0)),
                pl.BlockSpec((length, width), by_row),
                pl.BlockSpec((length, width), by_row),
                pl.BlockSpec((length, width), by_row),
                pl.BlockSpec((length, width), by_row),
                pl.BlockSpec((length, 128), by_row),
            ),
            scratch_shapes=[pltpu.VMEM((length // QB, QB, size), F32)],
        ),
        compiler_params=pltpu.CompilerParams(vmem_limit_bytes=56 * MIB),
        name="attend",
    )(place, inputs, segment_ids.reshape(rows, 1, length), wt, wo, small, gains, shifts, ranges)


def feed_kernel(
    place, nq_ref, xh_hbm, inv_ref, cot_hbm, w1_ref, w2_ref, small_ref, gains, shifts, ranges,
    out_ref, g2_ref, g1_ref, da_ref, dh1_ref, sums_ref, gb1_ref,
    gq, factor, total, dl, xh, cot, dh2, do, load_sem,
):
    i = pl.program_id(0)
    tokens, width = nq_ref.shape
    blocks = tokens // QB
    shards = gq.shape[0]
    shard = place[1 + i % shards]

    def copies():
        return (
            pltpu.make_async_copy(xh_hbm, xh, load_sem.at[0]),
            pltpu.make_async_copy(
                cot_hbm.at[pl.ds(pl.multiple_of(place[0] * tokens, QB), tokens)], cot, load_sem.at[1]
            ),
        )

    @pl.when(i == 0)
    def _():
        for copy in copies():
            copy.start()
        total[...] = jnp.zeros_like(total)

    @pl.when(i < shards)
    def _():
        def block(b, _):
            rows = pl.ds(pl.multiple_of(b * QB, QB), QB)
            pre = dot_nn(nq_ref[rows], w1_ref[0]) + small_ref[0, 0:1]
            cdf = 0.5 * (1.0 + lax.erf(pre * ROOT_HALF))
            coded, squash = quantize(pre * cdf, ranges[3])
            slope = cdf + pre * jnp.exp(-0.5 * pre * pre) * INV_ROOT_TWO_PI
            factor[i, rows] = ((1.0 - squash * squash) * slope).astype(BF16)
            coded = coded.astype(BF16)
            gq[i, rows] = coded
            total[rows] += dot_nn(coded, w2_ref[0])
            return 0

        lax.fori_loop(0, blocks, block, 0)

    @pl.when(i == shards - 1)
    def _():
        for copy in copies():
            copy.wait()
        sums_ref[...] = jnp.zeros_like(sums_ref)

        def block(b, _):
            rows = pl.ds(pl.multiple_of(b * QB, QB), QB)
            first = xh[rows] * gains[0:1] + shifts[1:2]
            normed, inverse = norm(first + total[rows] + shifts[2:3])
            out_ref[rows] = normed * gains[1:2] + shifts[3:4]
            grad = cot[rows]
            back = norm_back(grad * gains[1:2], normed, inverse)
            dh2[rows] = back
            do[rows] = back.astype(BF16)
            sums_ref[1:2] += jnp.sum(grad * normed, 0, keepdims=True)
            sums_ref[4:5] += jnp.sum(back, 0, keepdims=True)
            sums_ref[5:6] += jnp.sum(grad, 0, keepdims=True)
            return 0

        lax.fori_loop(0, blocks, block, 0)
        total[...] = jnp.zeros_like(total)

    @pl.when(i >= shards)
    def _():
        def block(b, _):
            rows = pl.ds(pl.multiple_of(b * QB, QB), QB)
            back = dot_nt(do[rows], w2_ref[0]) * factor[i - shards, rows].astype(F32)
            low = back.astype(BF16)
            dl[rows] = low
            total[rows] += dot_nt(low, w1_ref[0])
            return jnp.sum(back, 0, keepdims=True)

        acc = block(0, 0)
        acc = lax.fori_loop(1, blocks, lambda b, a: a + block(b, 0), acc)

        @pl.when(i < shards + 2)
        def _():
            gb1_ref[0] = jnp.broadcast_to(acc, gb1_ref.shape[1:])
            g2_ref[0] = dot_tn(gq[i - shards], do[...]).astype(BF16)
            g1_ref[0] = dot_tn(nq_ref[...], dl[...]).astype(BF16)

    @pl.when(i == 2 * shards - 1)
    def _():
        def block(b, _):
            rows = pl.ds(pl.multiple_of(b * QB, QB), QB)
            normed = xh[rows]
            squash = jnp.tanh((normed * gains[0:1] + shifts[1:2]) * (1.0 / ranges[2]))
            grad = dh2[rows] + total[rows] * (1.0 - squash * squash)
            inverse = jnp.max(inv_ref[rows], axis=1, keepdims=True)
            back = norm_back(grad * gains[0:1], normed, inverse)
            dh1_ref[rows] = back
            da_ref[rows] = back.astype(BF16)
            sums_ref[0:1] += jnp.sum(grad * normed, 0, keepdims=True)
            sums_ref[2:3] += jnp.sum(back, 0, keepdims=True)
            sums_ref[3:4] += jnp.sum(grad, 0, keepdims=True)
            return 0

        lax.fori_loop(0, blocks, block, 0)


def feed(place, nq, xh, inv, cotangent, w1, w2, small, gains, shifts, ranges):
    tokens, width = nq.shape
    shards, _, hidden = w1.shape
    one = pl.Buffered(1)
    fixed = lambda shape: pl.BlockSpec(shape, lambda i, place: (0,) * len(shape), pipeline_mode=one)
    ours = lambda i, place: (jnp.clip(i - shards, 0, 1), 0, 0)
    turn = lambda i, place: (place[1 + i % shards], 0, 0)
    return pl.pallas_call(
        feed_kernel,
        out_shape=(
            S((tokens, width), F32),
            S((2, hidden, width), BF16),
            S((2, width, hidden), BF16),
            S((tokens, width), BF16),
            S((tokens, width), F32),
            S((8, width), F32),
            S((2, 8, hidden), F32),
        ),
        grid_spec=pltpu.PrefetchScalarGridSpec(
            num_scalar_prefetch=1,
            grid=(2 * shards,),
            in_specs=[
                fixed(nq.shape),
                ANY,
                fixed(inv.shape),
                ANY,
                pl.BlockSpec((1, width, hidden), turn),
                pl.BlockSpec((1, hidden, width), turn),
                pl.BlockSpec((1, 8, width), turn),
                fixed(gains.shape),
                fixed(shifts.shape),
                SMEM,
            ],
            out_specs=(
                fixed((tokens, width)),
                pl.BlockSpec((1, hidden, width), ours),
                pl.BlockSpec((1, width, hidden), ours),
                fixed((tokens, width)),
                fixed((tokens, width)),
                fixed((8, width)),
                pl.BlockSpec((1, 8, hidden), ours),
            ),
            scratch_shapes=[
                pltpu.VMEM((shards, tokens, hidden), BF16),
                pltpu.VMEM((shards, tokens, hidden), BF16),
                pltpu.VMEM((tokens, width), F32),
                pltpu.VMEM((tokens, hidden), BF16),
                pltpu.VMEM((tokens, width), F32),
                pltpu.VMEM((tokens, width), F32),
                pltpu.VMEM((tokens, width), F32),
                pltpu.VMEM((tokens, width), BF16),
                pltpu.SemaphoreType.DMA((2,)),
            ],
        ),
        compiler_params=pltpu.CompilerParams(vmem_limit_bytes=60 * MIB),
        name="feed",
    )(place, nq, xh, inv, cotangent, w1, w2, small, gains, shifts, ranges)


def attend_back_kernel(
    place, x_ref, xq_ref, q_ref, k_ref, v_ref, p_ref, cq_ref, cs_ref, da_ref, dh1_ref, wt_ref, wo_ref,
    ranges, dx_ref, go_ref, gq_ref, gb_ref, dc, dq, dk, dv, acc_o, acc_q,
):
    r = pl.program_id(0)
    length, width = x_ref.shape
    wins = windows(length)
    side = width // 2
    mine = pl.ds(pl.multiple_of(place[1] // 2 * side, 128), side)
    dc[...] = (dot_nt(da_ref[...], wo_ref[...]) * cs_ref[...].astype(F32)).astype(BF16)
    lanes = lax.broadcasted_iota(jnp.int32, (QB, 128), 1) < HD

    def pair(p, _):
        at = pl.ds(pl.multiple_of(p * 128, 128), 128)
        d_keys, d_values = [], []
        for b, (first, low, size) in enumerate(wins):
            wide = lax.broadcasted_iota(jnp.int32, (size, 128), 1) < HD
            queries = q_ref[first : first + QB, at]
            keys = k_ref[low : low + size, at]
            values = v_ref[low : low + size, at]
            context = dc[first : first + QB, at]
            got = []
            for head in range(2):
                own = lanes if head == 0 else jnp.logical_not(lanes)
                chosen = jnp.where(own, context.astype(F32), 0.0).astype(BF16)
                probs = p_ref[2 * p + head, first : first + QB, 0:size]
                d_probs = dot_nt(chosen, values)
                exact = probs.astype(F32)
                both = exact * d_probs
                d_low = (both - exact * jnp.sum(both, -1, keepdims=True)).astype(BF16)
                got.append(
                    (dot_nn(d_low, keys), dot_tn(d_low, queries), dot_tn(probs, context))
                )
            dq[first : first + QB, at] = (jnp.where(lanes, got[0][0], got[1][0]) * 0.125).astype(BF16)
            d_keys.append(jnp.where(wide, got[0][1], got[1][1]))
            d_values.append(jnp.where(wide, got[0][2], got[1][2]))
        for ref, parts, scale in ((dk, d_keys, 0.125), (dv, d_values, 1.0)):
            for lane in range(0, length, SPAN):
                terms = [
                    part[lane - low : lane - low + SPAN]
                    for part, (_, low, size) in zip(parts, wins)
                    if low <= lane < low + size
                ]
                ref[lane : lane + SPAN, at] = (sum(terms[1:], terms[0]) * scale).astype(BF16)
        return 0

    lax.fori_loop(0, width // 128, pair, 0)
    squash = jnp.tanh(x_ref[...] * (1.0 / ranges[0]))
    back = dot_nn(dq[...], wt_ref[0]) + dot_nn(dk[...], wt_ref[1]) + dot_nn(dv[...], wt_ref[2])
    dx_ref[...] = dh1_ref[...] + back * (1.0 - squash * squash)

    def sums(ref):
        return jnp.sum(ref[:, mine].astype(F32), 0, keepdims=True)

    @pl.when(r == 0)
    def _():
        acc_o[...] = jnp.zeros_like(acc_o)
        acc_q[...] = jnp.zeros_like(acc_q)
        gb_ref[...] = jnp.zeros_like(gb_ref)

    acc_o[...] += dot_tn(cq_ref[:, mine], da_ref[...])
    for j, ref in enumerate((dq, dk, dv)):
        acc_q[j] += dot_tn(ref[:, mine], xq_ref[...])
    gb_ref[0:1] += sums(dq)
    gb_ref[1:2] += sums(dv)

    @pl.when(r == pl.num_programs(0) - 1)
    def _():
        go_ref[...] = acc_o[...].astype(BF16)
        gq_ref[...] = acc_q[...].astype(BF16)


def attend_back(place, inputs, xq, q, k, v, probs, cq, cs, da, dh1, wt, wo, ranges, rows, length):
    tokens, width = inputs.shape
    mine = rows // 2
    half = tokens // 2
    size = probs.shape[2]
    side = width // 2
    by_row = lambda r, place: (r, 0)
    whole = lambda n: (lambda r, place: (0,) * n)
    one = pl.Buffered(1)
    return pl.pallas_call(
        attend_back_kernel,
        out_shape=(
            S((half, width), F32),
            S((side, width), BF16),
            S((3, side, width), BF16),
            S((8, side), F32),
        ),
        grid_spec=pltpu.PrefetchScalarGridSpec(
            num_scalar_prefetch=1,
            grid=(mine,),
            in_specs=[
                pl.BlockSpec((length, width), lambda r, place: (place[0] * mine + r, 0)),
                *[pl.BlockSpec((length, width), by_row)] * 4,
                pl.BlockSpec((width // HD, length, size), lambda r, place: (r, 0, 0)),
                *[pl.BlockSpec((length, width), by_row)] * 4,
                pl.BlockSpec(wt.shape, whole(3), pipeline_mode=one),
                pl.BlockSpec(wo.shape, whole(2), pipeline_mode=one),
                SMEM,
            ],
            out_specs=(
                pl.BlockSpec((length, width), by_row),
                pl.BlockSpec((side, width), whole(2), pipeline_mode=one),
                pl.BlockSpec((3, side, width), whole(3), pipeline_mode=one),
                pl.BlockSpec((8, side), whole(2)),
            ),
            scratch_shapes=[
                pltpu.VMEM((length, width), BF16),
                pltpu.VMEM((length, width), BF16),
                pltpu.VMEM((length, width), BF16),
                pltpu.VMEM((length, width), BF16),
                pltpu.VMEM((side, width), F32),
                pltpu.VMEM((3, side, width), F32),
            ],
        ),
        compiler_params=pltpu.CompilerParams(vmem_limit_bytes=60 * MIB),
        name="attend_back",
    )(place, inputs, xq, q, k, v, probs, cq, cs, da, dh1, wt, wo, ranges)


CHUNK = 192


def reduce_kernel(
    extra, g2, g1, go, gq, smalls, lo_half, dx_half,
    result, small_out, lo_full, dx_full,
    mine, theirs, got_core, own, got_y, part, got_1, got_2, got_x, small_own, small_got,
    load_sem, core_send, core_recv, y_send, y_recv, z1_send, z1_recv, z2_send, z2_recv,
    x_send, x_recv, z3_send, z3_recv, ag_send, ag_recv, big_sem, big_send, big_recv,
    small_send, small_recv,
):
    t, d = lax.axis_index("tensor"), lax.axis_index("dp")
    c = t % 2
    y = d % 2
    z = (d // 2) % 4
    end = jnp.logical_or(z == 0, z == 3)
    middle = jnp.logical_not(end)
    sib = (d, flip(t, 1))
    side = (flip(d, 1), t)
    inner = (flip(d, 2), t)
    across = (d - 2 * z + 2 * (3 - z), t)
    others = [(flip(d, 8 << b), t) for b in range(extra)]
    rows, width = own.shape
    chunks = rows // CHUNK
    half = CHUNK // 2

    barrier = pltpu.get_barrier_semaphore()
    peers = [sib, side, inner, across] + others
    for peer in peers:
        pl.semaphore_signal(barrier, inc=1, device_id=peer, device_id_type=MESH)
    pl.semaphore_wait(barrier, len(peers))

    def remote(src, dst, send, recv, to):
        return pltpu.make_async_remote_copy(
            src_ref=src, dst_ref=dst, send_sem=send, recv_sem=recv, device_id=to, device_id_type=MESH
        )

    tokens = lo_half.shape[0]
    at = pl.ds(pl.multiple_of(c * tokens, 256), tokens)
    big = []
    for i, (src, dst) in enumerate(((lo_half, lo_full), (dx_half, dx_full))):
        copy = pltpu.make_async_copy(src, dst.at[at], big_sem.at[i])
        copy.start()
        other = remote(src, dst.at[at], big_send.at[i], big_recv.at[i], sib)
        other.start()
        big += [copy, other]

    loads = []
    hidden = g2.shape[1]
    cols = go.shape[0] // 2
    for which, (buffer, core) in enumerate(((mine, c), (theirs, 1 - c))):
        places = [
            (g2.at[core], buffer.at[0:hidden]),
            (g1.at[core], buffer.at[hidden : 2 * hidden]),
            (
                go.at[pl.ds(pl.multiple_of(core * cols, 16), cols)],
                buffer.at[2 * hidden : 2 * hidden + cols],
            ),
        ]
        for j in range(3):
            base = 2 * hidden + (j + 1) * cols
            places.append(
                (
                    gq.at[j, pl.ds(pl.multiple_of(core * cols, 16), cols)],
                    buffer.at[base : base + cols],
                )
            )
        for i, (src, dst) in enumerate(places):
            copy = pltpu.make_async_copy(src, dst, load_sem.at[which * 6 + i])
            copy.start()
            loads.append(copy)
    for copy in loads:
        copy.wait()

    small_own[...] = smalls[...]
    steps = [sib, side, inner, across] + others
    for i, peer in enumerate(steps):
        copy = remote(small_own, small_got.at[i], small_send.at[i], small_recv.at[i], peer)
        copy.start()
        copy.wait()
        small_own[...] = small_own[...] + small_got[i]
    small_out[...] = small_own[...]

    def span(k):
        return pl.ds(k * CHUNK, CHUNK)

    def part_of(k, which):
        return pl.ds(pl.multiple_of(k * CHUNK + which * half, 16), half)

    def core_copy(k):
        return remote(theirs.at[span(k)], got_core.at[span(k)], core_send.at[k], core_recv.at[k], sib)

    def y_copy(k):
        return remote(own.at[part_of(k, 1 - y)], got_y.at[k], y_send.at[k], y_recv.at[k], side)

    def z1_copy(k):
        return remote(part.at[k], got_1.at[k], z1_send.at[k], z1_recv.at[k], inner)

    def z2_copy(k):
        return remote(part.at[k], got_2.at[k], z2_send.at[k], z2_recv.at[k], across)

    def x_copy(k, b):
        return remote(part.at[k], got_x.at[b, k], x_send.at[b, k], x_recv.at[b, k], others[b])

    def z3_copy(k):
        there = result.at[part_of(k, y)]
        return remote(there, there, z3_send.at[k], z3_recv.at[k], inner)

    def ag_copy(k):
        there = result.at[part_of(k, y)]
        return remote(there, there, ag_send.at[k], ag_recv.at[k], side)

    def stage(s, k):
        if s == 0:
            core_copy(k).start()
        if s == 1:
            core_copy(k).wait()
            own[span(k)] = (mine[span(k)].astype(F32) + got_core[span(k)].astype(F32)).astype(BF16)
            y_copy(k).start()
        if s == 2:
            y_copy(k).wait()
            part[k] = (own[part_of(k, y)].astype(F32) + got_y[k].astype(F32)).astype(BF16)

            @pl.when(end)
            def _():
                z1_copy(k).start()

        if s == 3:

            @pl.when(middle)
            def _():
                z1_copy(k).wait_recv()
                part[k] = (part[k].astype(F32) + got_1[k].astype(F32)).astype(BF16)
                z2_copy(k).start()

        if s == 4:

            @pl.when(middle)
            def _():
                z2_copy(k).wait()
                part[k] = (part[k].astype(F32) + got_2[k].astype(F32)).astype(BF16)
                for b in range(extra):
                    copy = x_copy(k, b)
                    copy.start()
                    copy.wait()
                    part[k] = (part[k].astype(F32) + got_x[b, k].astype(F32)).astype(BF16)
                result[part_of(k, y)] = part[k]
                z3_copy(k).start()
                ag_copy(k).start()

        if s == 5:

            @pl.when(end)
            def _():
                z3_copy(k).wait_recv()
                ag_copy(k).start()

        if s == 6:
            ag_copy(k).wait()

            @pl.when(end)
            def _():
                z1_copy(k).wait_send()

            @pl.when(middle)
            def _():
                z3_copy(k).wait_send()

    for step in range(chunks + 6):
        for s in range(7):
            if 0 <= step - s < chunks:
                stage(s, step - s)
    for copy in big:
        copy.wait()


def reduce_grads(nd, g2, g1, go, gq, smalls, lo_half, dx_half):
    hidden, width = g2.shape[1:]
    cols = go.shape[0] // 2
    rows = 2 * hidden + 4 * cols
    chunks = rows // CHUNK
    half = CHUNK // 2
    extra = (nd // 8).bit_length() - 1
    tokens = lo_half.shape[0]
    dma = pltpu.SemaphoreType.DMA
    buf = lambda *shape: pltpu.VMEM(shape, BF16)
    count = max(extra, 1)
    return pl.pallas_call(
        functools.partial(reduce_kernel, extra),
        out_shape=(
            S((rows, width), BF16),
            S(smalls.shape, F32),
            S((2 * tokens, width), F32),
            S((2 * tokens, width), F32),
        ),
        in_specs=[ANY] * 4 + [VMEM] + [ANY] * 2,
        out_specs=(VMEM, VMEM, ANY, ANY),
        scratch_shapes=[
            buf(rows, width), buf(rows, width), buf(rows, width), buf(rows, width),
            buf(chunks, half, width), buf(chunks, half, width),
            buf(chunks, half, width), buf(chunks, half, width), buf(count, chunks, half, width),
            pltpu.VMEM(smalls.shape, F32),
            pltpu.VMEM((4 + extra,) + smalls.shape, F32),
            dma((12,)),
            dma((chunks,)), dma((chunks,)), dma((chunks,)), dma((chunks,)),
            dma((chunks,)), dma((chunks,)), dma((chunks,)), dma((chunks,)),
            dma((count, chunks)), dma((count, chunks)),
            dma((chunks,)), dma((chunks,)), dma((chunks,)), dma((chunks,)),
            dma((2,)), dma((2,)), dma((2,)),
            dma((4 + extra,)), dma((4 + extra,)),
        ],
        compiler_params=pltpu.CompilerParams(
            collective_id=2, has_side_effects=True, vmem_limit_bytes=60 * MIB
        ),
        name="reduce_grads",
    )(g2, g1, go, gq, smalls, lo_half, dx_half)


def per_device(
    nd, inputs, segment_ids, w_qkv, b_qv, w_out, w_ff1, b_ff1, w_ff2, norm_gains, shift_biases,
    act_ranges, cotangent,
):
    t = lax.axis_index("tensor")
    c, pair = t % 2, t // 2
    rows, length = segment_ids.shape
    width = inputs.shape[1]
    cols = w_qkv.shape[2]
    hidden = w_ff1.shape[1]
    order = [(2 * pair + i) % 4 for i in range(4)]
    place = jnp.stack([c] + order).astype(jnp.int32)
    wt, wo, w1, w2, small = gather_weights(w_qkv, w_out, w_ff1, w_ff2, b_qv, b_ff1)
    weight_max = jnp.max(small[:, 3, ::128], axis=0)
    xq, q, k, v, probs, cq, cs, nq, xh, inv = attend(
        place, inputs, segment_ids, wt, wo, small, norm_gains, shift_biases, act_ranges
    )
    lo_half, g2, g1, da, dh1, sums, gb1 = feed(
        place, nq, xh, inv, cotangent, w1, w2, small, norm_gains, shift_biases, act_ranges
    )
    dx_half, go, gq, gb = attend_back(
        place, inputs, xq, q, k, v, probs, cq, cs, da, dh1, wt, wo, act_ranges, rows, length
    )
    smalls = jnp.concatenate(
        [sums[:6], gb1[:, 0], jnp.pad(gb[:2], ((0, 6), (0, width - gb.shape[1])))], axis=0
    )
    grads, smalls, layer_out, input_grad = reduce_grads(nd, g2, g1, go, gq, smalls, lo_half, dx_half)
    grads = grads.astype(F32)
    grad_ff2 = grads[:hidden]
    grad_ff1 = grads[hidden : 2 * hidden]
    grad_out = grads[2 * hidden : 2 * hidden + cols]
    grad_qkv = grads[2 * hidden + cols :].reshape(3, cols, width).transpose(0, 2, 1)
    share = lax.dynamic_slice_in_dim(smalls[:6], t * cols, cols, 1)
    grad_gains, grad_shifts = share[:2], share[2:6]
    grad_bff1 = lax.dynamic_slice_in_dim(smalls, 6 + c, 1, 0)[0]
    grad_bqv = lax.dynamic_slice_in_dim(smalls[8:10], c * cols, cols, 1)
    return (
        layer_out, input_grad, grad_qkv, grad_bqv, grad_out, grad_ff1, grad_bff1, grad_ff2,
        grad_gains, grad_shifts, weight_max,
    )


def solution(mesh):
    return jax.shard_map(
        functools.partial(per_device, mesh.shape["dp"]),
        mesh=mesh,
        in_specs=(
            P("dp", None),
            P("dp", None),
            P(None, None, "tensor"),
            P(None, "tensor"),
            P("tensor", None),
            P(None, "tensor"),
            P("tensor"),
            P("tensor", None),
            P(),
            P(),
            P(),
            P("dp", None),
        ),
        out_specs=(
            P("dp", None),
            P("dp", None),
            P(None, None, "tensor"),
            P(None, "tensor"),
            P("tensor", None),
            P(None, "tensor"),
            P("tensor"),
            P("tensor", None),
            P(None, "tensor"),
            P(None, "tensor"),
            P(),
        ),
        check_vma=False,
    )
```

time: 835 us -> 440 us (0.53); the launches traced: 825 us -> 439 us
  Pallas kernels: 0 us -> 411 us
  waiting for transfers between devices: 385 us -> 0 us
  matrix products: 235 us -> 0 us
  other arithmetic: 86.7 us -> 1.16 us
  blocking collectives: 45.4 us -> 0 us
  local copies, waits for them, and re-layouts: 50.4 us -> 26 us
  between operations: 20.9 us -> 0.82 us
    pallas_call x0 -> x5, Pallas kernels: none -> 411 us  [the longest x1 200 us: reduce_grads(): pl.pallas_call(functools.partial(reduce_kernel, extra), out_shape=(S((row...]
    psum x5 -> x0, waiting for transfers between devices: 385 us -> none  [the longest x1 229 us: per_device(): lax.psum((grad_qkv, grad_bqv, grad_out, grad_ff1, grad_bff1, grad_ff2, gr...]
    dot_general x40 -> x0, matrix products: 235 us -> none  [the longest x1 49.8 us: per_device(): pre = jnp.dot(n_low, ff1_low, preferred_element_type=jnp.float32) + b_ff1]
    psum x1 -> x0, blocking collectives: 37.1 us -> none  [per_device(): lax.psum((grad_qkv, grad_bqv, grad_out, grad_ff1, grad_bff1, grad_ff2, gr...]
    reduce_sum x13 -> x0, other arithmetic: 36.4 us -> none  [the longest x1 9.69 us: per_device(): jnp.sum(d_first * normed1, 0)]
    convert_element_type x7 -> x0, other arithmetic: 24.4 us -> none  [the longest x1 9.93 us: stair_act(): return (result.astype(jnp.bfloat16), slopes)]
    unnamed x104 -> x17, local copies, waits for them, and re-layouts: 22.4 us -> 11.7 us
    add x1 -> x0, other arithmetic: 9.64 us -> none  [per_device(): input_grad = d_res1 + d_x * x_slope]
  transfers between devices with their start and end apart: 5 -> 0, of which waited for: 4 -> 0; matrix products, arithmetic and copies ran while one was open for 11% -> 0% of each run, Pallas kernels for 0% -> 0%
where the time goes in v1:
time: 440 us; the launch traced here: 439 us
  Pallas kernels  411 us (93%)
  local copies, waits for them, and re-layouts  26 us (6%)
    pallas_call x1, Pallas kernels, reduce_grads(): pl.pallas_call(functools.partial(reduce_kernel, extra), out_shape=(S((row...  200 us
    pallas_call x1, Pallas kernels, gather_weights(): pl.pallas_call(gather_kernel, out_shape=(S((3, shards * cols, width), BF1...  68.2 us
    pallas_call x1, Pallas kernels, feed(): pl.pallas_call(feed_kernel, out_shape=(S((tokens, width), F32), S((2, hid...  58.9 us
    pallas_call x1, Pallas kernels, attend_back(): pl.pallas_call(attend_back_kernel, out_shape=(S((half, width), F32), S((s...  45.8 us
    pallas_call x1, Pallas kernels, attend(): pl.pallas_call(attend_kernel, out_shape=(S((half, width), BF16), S((half,...  39 us
    unnamed x17, local copies, waits for them, and re-layouts  11.7 us

profile of v1, /device:TPU:0, one launch (start us, length us, event | category | flops | bytes accessed | tf_op | source)
XLA Modules:
  0.0 439.3 jit_solution(11566840259973410760)
XLA Ops:
  0.6 0.0 copy-start.4
  0.7 0.7 stack.23.place
  1.4 2.9 copy.23.wqkv
  4.4 0.0 copy-done.4
  4.4 0.6 reshape.32.bff1
  4.9 0.0 copy-start.3
  4.9 68.2 %gather_weights.1 = (bf16[3,768,768]{2,1,0:T(8,128)(2,1)}, bf16[768,768]{1,0:T(8,128)(2,1)}, bf16[4,768,768]{2,1,0:T(8,128)(2,1)}, bf16[4,768,768]{2,1,0:T(8,128)(2,1)}, f32[4,8,768]{2,1,0:T(8,128)}) custom-call(f32[3,768,192]{2,1,0:T(8,128)} %copy.23.wqkv, f32[192,768]{1,0:T(8,128)} %wout.1, f32[768,768]{1,0:T(8,128)} %wff1.1, f32[768,768]{1,0:T(8,128)} %wff2.1, ...), custom_call_target="tpu_custom_call" | custom-call | tf_op jit(solution)/shard_map/gather_weights/pallas_call | solution.py:233
  73.2 0.0 copy-done.3
  73.2 0.6 reshape.31.seg_ref
  73.8 39.0 %attend.1 = (bf16[1024,768]{1,0:T(8,128)(2,1)}, bf16[1024,768]{1,0:T(8,128)(2,1)}, bf16[1024,768]{1,0:T(8,128)(2,1)}, bf16[1024,768]{1,0:T(8,128)(2,1)}, bf16[24...) custom-call(s32[5]{0:T(128)} %stack.23.place, ...), custom_call_target="tpu_custom_call" | custom-call | tf_op jit(solution)/shard_map/attend/pallas_call | solution.py:330
  112.8 58.9 %feed.1 = (f32[1024,768]{1,0:T(8,128)}, bf16[2,768,768]{2,1,0:T(8,128)(2,1)}, bf16[2,768,768]{2,1,0:T(8,128)(2,1)}, bf16[1024,768]{1,0:T(8,128)(2,1)}, f32[1024,...) custom-call(s32[5]{0:T(128)} %stack.23.place, bf16[1024,768]{1,0:T(8,128)(2,1)} %get-tuple-element.44.nq_ref, ...), custom_call_target="tpu_custom_call" | custom-call | tf_op jit(solution)/shard_map/feed/pallas_call | solution.py:485
  171.6 0.0 copy-start.1
  171.7 0.0 copy-start.2
  171.7 45.8 %attend_back.1 = (f32[1024,768]{1,0:T(8,128)}, bf16[384,768]{1,0:T(8,128)(2,1)}, bf16[3,384,768]{2,1,0:T(8,128)(2,1)}, f32[8,384]{1,0:T(8,128)}) custom-call(s32[5]{0:T(128)} %stack.23.place, f32[2048,768]{1,0:T(8,128)} %x_ref.3, bf16[1024,768]{1,0:T(8,128)(2,1)} %get-tuple-element.51.xq_ref, bf16[1024,768]{1,0:T(8,128)(2,1)} %get-tuple-element.52.q_ref, ...), custom_call_target="tpu_custom_call" | custom-call | tf_op jit(solution)/shard_map/attend_back/pallas_call | solution.py:618
  217.4 0.7 slice.38
  218.2 0.0 copy-done.1
  218.2 0.0 copy-done.2
  218.2 0.6 select_maximum_fusion.smalls
  218.8 199.6 %reduce_grads.1 = (bf16[2304,768]{1,0:T(8,128)(2,1)}, f32[16,768]{1,0:T(8,128)}, f32[2048,768]{1,0:T(8,128)}, f32[2048,768]{1,0:T(8,128)}) custom-call(bf16[2,768,768]{2,1,0:T(8,128)(2,1)} %get-tuple-element.49.g2, bf16[2,768,768]{2,1,0:T(8,128)(2,1)} %get-tuple-element.50.g1, bf16[384,768]{1,0:T(8,128)(2,1)} %get-tuple-element.60.go, ...), custom_call_target="tpu_custom_call" | custom-call | tf_op jit(solution)/shard_map/reduce_grads/pallas_call | solution.py:845
  418.4 0.7 slice.44
  419.1 0.7 slice.40
  419.9 0.7 constant_dynamic-slice_fusion
  420.5 0.0 copy-start
  420.5 4.3 fusion
  424.9 0.0 copy-done
  424.9 1.3 slice.49
  426.2 0.0 slice-start
  426.2 0.9 slice.50
  427.1 0.7 dynamic-slice.1
  427.7 1.3 dynamic-slice_reduce_fusion
  429.1 1.0 slice.47
  430.0 0.5 reduce_max.9
  430.6 0.0 slice-start.1
  430.6 6.1 %copy.27 = f32[2048,768]{1,0:T(8,128)} copy(f32[2048,768]{1,0:T(8,128)} %get-tuple-element.86) | data formatting | bytes 12582912
  436.6 0.0 slice-done
  436.6 0.0 slice-done.1
  436.6 2.7 copy.28
  (3 shorter events, 0.0 us)
Async XLA Ops:
  0.6 3.7 copy-start.4
  4.9 68.2 %copy-start.3 = (s32[4,512]{1,0:T(4,128)S(1)}, s32[4,512]{1,0:T(4,128)}, u32[]{:S(2)}) copy-start(s32[4,512]{1,0:T(4,128)} %param.13) | copy-start | bytes 24580
  171.6 46.5 %copy-start.1 = (f32[2,8,768]{2,1,0:T(8,128)S(1)}, f32[2,8,768]{2,1,0:T(8,128)}, u32[]{:S(2)}) copy-start(f32[2,8,768]{2,1,0:T(8,128)} %get-tuple-element.63) | copy-start | bytes 147460
  171.7 46.5 %copy-start.2 = (f32[8,768]{1,0:T(8,128)S(1)}, f32[8,768]{1,0:T(8,128)}, u32[]{:S(2)}) copy-start(f32[8,768]{1,0:T(8,128)} %get-tuple-element.62) | copy-start | bytes 73732
  420.5 4.3 copy-start
  426.2 10.4 %slice-start = ((s8[6291456]{0:T(1024)(128)(4,1)}), s8[2097152]{0:T(1024)(128)(4,1)S(1)}, s32[]{:S(2)}) async-start(s8[6291456]{0:T(1024)(128)(4,1)} %bitcast.11), calls=%async_computation | async-start | bytes 4194304
  430.6 6.1 %slice-start.1 = ((s8[6291456]{0:T(1024)(128)(4,1)}), s8[4194304]{0:T(1024)(128)(4,1)S(1)}, s32[]{:S(2)}) async-start(s8[6291456]{0:T(1024)(128)(4,1)} %bitcast.11), calls=%async_computation.1 | async-start | bytes 8388608

commit v2 on v1

--- a/solution.py
+++ b/solution.py
@@ -655,52 +655,255 @@
     )(place, inputs, xq, q, k, v, probs, cq, cs, da, dh1, wt, wo, ranges)
 
 
-CHUNK = 192
+GROUP = 192
+QUARTER = GROUP // 4
+HOPS = ("core", "y", "z1", "z2", "z3", "ag")
+LINE_HOPS = ("zs1", "zs2", "zy", "zb1", "zb2", "zb3")
+
+
+def sum_scratch(groups, width, extra, small_shape):
+    count = max(extra, 1)
+    dma = pltpu.SemaphoreType.DMA
+    buf = lambda *shape: pltpu.VMEM(shape + (width,), BF16)
+    kinds = dict(
+        own=buf(groups * GROUP), got_y=buf(groups, QUARTER), part=buf(groups, QUARTER),
+        got_1=buf(groups, QUARTER), got_2=buf(groups, QUARTER), got_x=buf(count, groups, QUARTER),
+        line_1=buf(groups, 2, QUARTER), line_2=buf(groups, 2, QUARTER), line_y=buf(groups, 2, QUARTER),
+        line_x=buf(count, groups, 2, QUARTER),
+        small_own=pltpu.VMEM(small_shape, F32), small_got=pltpu.VMEM((4 + extra,) + small_shape, F32),
+        x_s=dma((count, groups)), x_r=dma((count, groups)),
+        lx_s=dma((count, groups, 2)), lx_r=dma((count, groups, 2)),
+        small_s=dma((4 + extra,)), small_r=dma((4 + extra,)),
+    )
+    for hop in HOPS:
+        kinds[hop + "_s"], kinds[hop + "_r"] = dma((groups,)), dma((groups,))
+    for hop in LINE_HOPS:
+        kinds[hop + "_s"], kinds[hop + "_r"] = dma((groups, 2)), dma((groups, 2))
+    return list(kinds), list(kinds.values())
+
+
+class GradientSum:
+    STAGES = 7
+
+    def __init__(self, extra, mine, theirs, result, refs):
+        self.__dict__.update(refs)
+        self.extra, self.mine, self.theirs, self.result = extra, mine, theirs, result
+        t, d = lax.axis_index("tensor"), lax.axis_index("dp")
+        self.y = d % 2
+        self.z = (d // 2) % 4
+        self.end = jnp.logical_or(self.z == 0, self.z == 3)
+        self.middle = jnp.logical_not(self.end)
+        self.sib = (d, flip(t, 1))
+        self.side = (flip(d, 1), t)
+        self.inner = (flip(d, 2), t)
+        self.across = (d + 2 * (3 - 2 * self.z), t)
+        self.others = [(flip(d, 8 << b), t) for b in range(extra)]
+        self.peers = [self.sib, self.side, self.inner, self.across] + self.others
+        self.groups = self.own.shape[0] // GROUP
+
+    def enter(self):
+        barrier = pltpu.get_barrier_semaphore()
+        for peer in self.peers:
+            pl.semaphore_signal(barrier, inc=1, device_id=peer, device_id_type=MESH)
+        pl.semaphore_wait(barrier, len(self.peers))
+
+    def remote(self, src, dst, hop, at, to):
+        return pltpu.make_async_remote_copy(
+            src_ref=src, dst_ref=dst, send_sem=getattr(self, hop + "_s").at[at],
+            recv_sem=getattr(self, hop + "_r").at[at], device_id=to, device_id_type=MESH,
+        )
+
+    def small(self, i):
+        copy = self.remote(self.small_own, self.small_got.at[i], "small", i, self.peers[i])
+        return copy
+
+    def small_step(self, i):
+        if i > 0:
+            self.small(i - 1).wait()
+            self.small_own[...] = self.small_own[...] + self.small_got[i - 1]
+        if i < len(self.peers):
+            self.small(i).start()
+
+    def span(self, g):
+        return pl.ds(g * GROUP, GROUP)
+
+    def half(self, g, which):
+        return pl.ds(pl.multiple_of(g * GROUP + which * QUARTER, 16), QUARTER)
+
+    def line(self, g, i):
+        return pl.ds(g * GROUP + (2 + i) * QUARTER, QUARTER)
+
+    def core(self, g):
+        return self.remote(self.theirs.at[self.span(g)], self.own.at[self.span(g)], "core", g, self.sib)
+
+    def hop(self, name, g):
+        if name == "y":
+            return self.remote(self.own.at[self.half(g, 1 - self.y)], self.got_y.at[g], "y", g, self.side)
+        if name == "z1":
+            return self.remote(self.part.at[g], self.got_1.at[g], "z1", g, self.inner)
+        if name == "z2":
+            return self.remote(self.part.at[g], self.got_2.at[g], "z2", g, self.across)
+        there = self.result.at[self.half(g, self.y)]
+        return self.remote(there, there, name, g, self.inner if name == "z3" else self.side)
+
+    def line_hop(self, name, g, i):
+        mine = self.own.at[self.line(g, i)]
+        if name == "zs1":
+            return self.remote(mine, self.line_1.at[g, i], name, (g, i), self.inner)
+        if name == "zs2":
+            return self.remote(mine, self.line_2.at[g, i], name, (g, i), self.across)
+        if name == "zy":
+            return self.remote(mine, self.line_y.at[g, i], name, (g, i), self.side)
+        there = self.result.at[self.line(g, i)]
+        return self.remote(there, there, name, (g, i), self.across if name == "zb2" else self.inner)
+
+    def stage(self, s, g):
+        add = lambda a, b: (a.astype(F32) + b.astype(F32)).astype(BF16)
+        when = lambda condition, body: pl.when(condition)(body)
+        root = [self.z == 1, self.z == 2]
+        passer = [self.z == 2, self.z == 1]
+        near = [self.z == 0, self.z == 3]
+        far = [self.z == 3, self.z == 0]
+        if s == 0:
+            self.core(g).start()
+        if s == 1:
+            self.core(g).wait()
+            self.own[self.span(g)] = add(self.own[self.span(g)], self.mine[self.span(g)])
+            self.hop("y", g).start()
+            when(self.end, lambda: [self.line_hop("zs1", g, i).start() for i in range(2)] and None)
+        if s == 2:
+            self.hop("y", g).wait()
+            self.part[g] = add(self.own[self.half(g, self.y)], self.got_y[g])
+            when(self.end, lambda: self.hop("z1", g).start())
+            for i in range(2):
+
+                def gather(i=i):
+                    self.line_hop("zs1", g, i).wait_recv()
+                    rows = self.line(g, i)
+                    self.own[rows] = add(self.own[rows], self.line_1[g, i])
+                    when(passer[i], lambda: self.line_hop("zs2", g, i).start())
+
+                when(self.middle, gather)
+        if s == 3:
+
+            def middle():
+                self.hop("z1", g).wait_recv()
+                self.part[g] = add(self.part[g], self.got_1[g])
+                self.hop("z2", g).start()
+
+            when(self.middle, middle)
+            for i in range(2):
+
+                def at_root(i=i):
+                    self.line_hop("zs2", g, i).wait_recv()
+                    rows = self.line(g, i)
+                    self.own[rows] = add(self.own[rows], self.line_2[g, i])
+                    self.line_hop("zy", g, i).start()
+
+                when(root[i], at_root)
+        if s == 4:
+
+            def total():
+                self.hop("z2", g).wait()
+                self.part[g] = add(self.part[g], self.got_2[g])
+                for b in range(self.extra):
+                    copy = self.remote(self.part.at[g], self.got_x.at[b, g], "x", (b, g), self.others[b])
+                    copy.start()
+                    copy.wait()
+                    self.part[g] = add(self.part[g], self.got_x[b, g])
+                self.result[self.half(g, self.y)] = self.part[g]
+                self.hop("ag", g).start()
+                self.hop("z3", g).start()
+
+            when(self.middle, total)
+            for i in range(2):
+
+                def spread(i=i):
+                    self.line_hop("zy", g, i).wait()
+                    rows = self.line(g, i)
+                    self.own[rows] = add(self.own[rows], self.line_y[g, i])
+                    for b in range(self.extra):
+                        copy = self.remote(
+                            self.own.at[rows], self.line_x.at[b, g, i], "lx", (b, g, i), self.others[b]
+                        )
+                        copy.start()
+                        copy.wait()
+                        self.own[rows] = add(self.own[rows], self.line_x[b, g, i])
+                    self.result[rows] = self.own[rows]
+                    self.line_hop("zb2", g, i).start()
+                    self.line_hop("zb1", g, i).start()
+
+                when(root[i], spread)
+        if s == 5:
+
+            def outer():
+                self.hop("z3", g).wait_recv()
+                self.hop("ag", g).start()
+
+            when(self.end, outer)
+            for i in range(2):
+
+                def onward(i=i):
+                    self.line_hop("zb2", g, i).wait_recv()
+                    self.line_hop("zb3", g, i).start()
+
+                when(passer[i], onward)
+        if s == 6:
+            self.hop("ag", g).wait()
+            for i in range(2):
+                when(near[i], lambda i=i: self.line_hop("zb1", g, i).wait_recv())
+                when(far[i], lambda i=i: self.line_hop("zb3", g, i).wait_recv())
+
+                def sent_root(i=i):
+                    self.line_hop("zb1", g, i).wait_send()
+                    self.line_hop("zb2", g, i).wait_send()
+
+                def sent_passer(i=i):
+                    self.line_hop("zs2", g, i).wait_send()
+                    self.line_hop("zb3", g, i).wait_send()
+
+                when(root[i], sent_root)
+                when(passer[i], sent_passer)
+
+            def sent_end():
+                self.hop("z1", g).wait_send()
+                for i in range(2):
+                    self.line_hop("zs1", g, i).wait_send()
+
+            when(self.end, sent_end)
+            when(self.middle, lambda: self.hop("z3", g).wait_send())
+
+    def tick(self, n):
+        for s in reversed(range(self.STAGES)):
+            if 0 <= n - s < self.groups:
+                self.stage(s, n - s)
+
+    def ticks(self):
+        return self.groups + self.STAGES - 1
 
 
 def reduce_kernel(
-    extra, g2, g1, go, gq, smalls, lo_half, dx_half,
-    result, small_out, lo_full, dx_full,
-    mine, theirs, got_core, own, got_y, part, got_1, got_2, got_x, small_own, small_got,
-    load_sem, core_send, core_recv, y_send, y_recv, z1_send, z1_recv, z2_send, z2_recv,
-    x_send, x_recv, z3_send, z3_recv, ag_send, ag_recv, big_sem, big_send, big_recv,
-    small_send, small_recv,
+    extra, names, g2, g1, go, gq, smalls, lo_half, dx_half, result, small_out, lo_full, dx_full,
+    mine, theirs, bounce, load_sem, big_sem, big_send, big_recv, *refs,
 ):
     t, d = lax.axis_index("tensor"), lax.axis_index("dp")
     c = t % 2
-    y = d % 2
-    z = (d // 2) % 4
-    end = jnp.logical_or(z == 0, z == 3)
-    middle = jnp.logical_not(end)
-    sib = (d, flip(t, 1))
-    side = (flip(d, 1), t)
-    inner = (flip(d, 2), t)
-    across = (d - 2 * z + 2 * (3 - z), t)
-    others = [(flip(d, 8 << b), t) for b in range(extra)]
-    rows, width = own.shape
-    chunks = rows // CHUNK
-    half = CHUNK // 2
-
-    barrier = pltpu.get_barrier_semaphore()
-    peers = [sib, side, inner, across] + others
-    for peer in peers:
-        pl.semaphore_signal(barrier, inc=1, device_id=peer, device_id_type=MESH)
-    pl.semaphore_wait(barrier, len(peers))
-
-    def remote(src, dst, send, recv, to):
-        return pltpu.make_async_remote_copy(
-            src_ref=src, dst_ref=dst, send_sem=send, recv_sem=recv, device_id=to, device_id_type=MESH
-        )
-
+    engine = GradientSum(extra, mine, theirs, result, dict(zip(names, refs)))
+    engine.enter()
     tokens = lo_half.shape[0]
     at = pl.ds(pl.multiple_of(c * tokens, 256), tokens)
     big = []
+    bounces = []
     for i, (src, dst) in enumerate(((lo_half, lo_full), (dx_half, dx_full))):
-        copy = pltpu.make_async_copy(src, dst.at[at], big_sem.at[i])
+        copy = pltpu.make_async_copy(src, bounce.at[i], big_sem.at[i])
         copy.start()
-        other = remote(src, dst.at[at], big_send.at[i], big_recv.at[i], sib)
+        bounces.append((copy, pltpu.make_async_copy(bounce.at[i], dst.at[at], big_sem.at[i])))
+        other = pltpu.make_async_remote_copy(
+            src_ref=src, dst_ref=dst.at[at], send_sem=big_send.at[i], recv_sem=big_recv.at[i],
+            device_id=engine.sib, device_id_type=MESH,
+        )
         other.start()
-        big += [copy, other]
+        big.append(other)
 
     loads = []
     hidden = g2.shape[1]
@@ -726,107 +929,18 @@
             copy = pltpu.make_async_copy(src, dst, load_sem.at[which * 6 + i])
             copy.start()
             loads.append(copy)
+    engine.small_own[...] = smalls[...]
+    for into, out in bounces:
+        into.wait()
+        out.start()
+        big.append(out)
     for copy in loads:
         copy.wait()
-
-    small_own[...] = smalls[...]
-    steps = [sib, side, inner, across] + others
-    for i, peer in enumerate(steps):
-        copy = remote(small_own, small_got.at[i], small_send.at[i], small_recv.at[i], peer)
-        copy.start()
-        copy.wait()
-        small_own[...] = small_own[...] + small_got[i]
-    small_out[...] = small_own[...]
-
-    def span(k):
-        return pl.ds(k * CHUNK, CHUNK)
-
-    def part_of(k, which):
-        return pl.ds(pl.multiple_of(k * CHUNK + which * half, 16), half)
-
-    def core_copy(k):
-        return remote(theirs.at[span(k)], got_core.at[span(k)], core_send.at[k], core_recv.at[k], sib)
-
-    def y_copy(k):
-        return remote(own.at[part_of(k, 1 - y)], got_y.at[k], y_send.at[k], y_recv.at[k], side)
-
-    def z1_copy(k):
-        return remote(part.at[k], got_1.at[k], z1_send.at[k], z1_recv.at[k], inner)
-
-    def z2_copy(k):
-        return remote(part.at[k], got_2.at[k], z2_send.at[k], z2_recv.at[k], across)
-
-    def x_copy(k, b):
-        return remote(part.at[k], got_x.at[b, k], x_send.at[b, k], x_recv.at[b, k], others[b])
-
-    def z3_copy(k):
-        there = result.at[part_of(k, y)]
-        return remote(there, there, z3_send.at[k], z3_recv.at[k], inner)
-
-    def ag_copy(k):
-        there = result.at[part_of(k, y)]
-        return remote(there, there, ag_send.at[k], ag_recv.at[k], side)
-
-    def stage(s, k):
-        if s == 0:
-            core_copy(k).start()
-        if s == 1:
-            core_copy(k).wait()
-            own[span(k)] = (mine[span(k)].astype(F32) + got_core[span(k)].astype(F32)).astype(BF16)
-            y_copy(k).start()
-        if s == 2:
-            y_copy(k).wait()
-            part[k] = (own[part_of(k, y)].astype(F32) + got_y[k].astype(F32)).astype(BF16)
-
-            @pl.when(end)
-            def _():
-                z1_copy(k).start()
-
-        if s == 3:
-
-            @pl.when(middle)
-            def _():
-                z1_copy(k).wait_recv()
-                part[k] = (part[k].astype(F32) + got_1[k].astype(F32)).astype(BF16)
-                z2_copy(k).start()
-
-        if s == 4:
-
-            @pl.when(middle)
-            def _():
-                z2_copy(k).wait()
-                part[k] = (part[k].astype(F32) + got_2[k].astype(F32)).astype(BF16)
-                for b in range(extra):
-                    copy = x_copy(k, b)
-                    copy.start()
-                    copy.wait()
-                    part[k] = (part[k].astype(F32) + got_x[b, k].astype(F32)).astype(BF16)
-                result[part_of(k, y)] = part[k]
-                z3_copy(k).start()
-                ag_copy(k).start()
-
-        if s == 5:
-
-            @pl.when(end)
-            def _():
-                z3_copy(k).wait_recv()
-                ag_copy(k).start()
-
-        if s == 6:
-            ag_copy(k).wait()
-
-            @pl.when(end)
-            def _():
-                z1_copy(k).wait_send()
-
-            @pl.when(middle)
-            def _():
-                z3_copy(k).wait_send()
-
-    for step in range(chunks + 6):
-        for s in range(7):
-            if 0 <= step - s < chunks:
-                stage(s, step - s)
+    for n in range(engine.ticks()):
+        if n <= len(engine.peers):
+            engine.small_step(n)
+        engine.tick(n)
+    small_out[...] = engine.small_own[...]
     for copy in big:
         copy.wait()
 
@@ -835,15 +949,12 @@
     hidden, width = g2.shape[1:]
     cols = go.shape[0] // 2
     rows = 2 * hidden + 4 * cols
-    chunks = rows // CHUNK
-    half = CHUNK // 2
     extra = (nd // 8).bit_length() - 1
     tokens = lo_half.shape[0]
     dma = pltpu.SemaphoreType.DMA
-    buf = lambda *shape: pltpu.VMEM(shape, BF16)
-    count = max(extra, 1)
+    names, scratch = sum_scratch(rows // GROUP, width, extra, smalls.shape)
     return pl.pallas_call(
-        functools.partial(reduce_kernel, extra),
+        functools.partial(reduce_kernel, extra, names),
         out_shape=(
             S((rows, width), BF16),
             S(smalls.shape, F32),
@@ -853,18 +964,12 @@
         in_specs=[ANY] * 4 + [VMEM] + [ANY] * 2,
         out_specs=(VMEM, VMEM, ANY, ANY),
         scratch_shapes=[
-            buf(rows, width), buf(rows, width), buf(rows, width), buf(rows, width),
-            buf(chunks, half, width), buf(chunks, half, width),
-            buf(chunks, half, width), buf(chunks, half, width), buf(count, chunks, half, width),
-            pltpu.VMEM(smalls.shape, F32),
-            pltpu.VMEM((4 + extra,) + smalls.shape, F32),
+            pltpu.VMEM((rows, width), BF16),
+            pltpu.VMEM((rows, width), BF16),
+            pltpu.VMEM((2, tokens, width), F32),
             dma((12,)),
-            dma((chunks,)), dma((chunks,)), dma((chunks,)), dma((chunks,)),
-            dma((chunks,)), dma((chunks,)), dma((chunks,)), dma((chunks,)),
-            dma((count, chunks)), dma((count, chunks)),
-            dma((chunks,)), dma((chunks,)), dma((chunks,)), dma((chunks,)),
             dma((2,)), dma((2,)), dma((2,)),
-            dma((4 + extra,)), dma((4 + extra,)),
+            *scratch,
         ],
         compiler_params=pltpu.CompilerParams(
             collective_id=2, has_side_effects=True, vmem_limit_bytes=60 * MIB

time: 440 us -> 341 us (0.78)
  Pallas kernels: 411 us -> 312 us
    pallas_call x1, Pallas kernels: 200 us -> 100 us  [reduce_grads(): pl.pallas_call(functools.partial(reduce_kernel, extra, names), out_shape=...]
where the time goes in v2:
time: 341 us; the launch traced here: 340 us
  Pallas kernels  312 us (91%)
  local copies, waits for them, and re-layouts  26 us (8%)
    pallas_call x1, Pallas kernels, reduce_grads(): pl.pallas_call(functools.partial(reduce_kernel, extra, names), out_shape=...  100 us
    pallas_call x1, Pallas kernels, gather_weights(): pl.pallas_call(gather_kernel, out_shape=(S((3, shards * cols, width), BF1...  68.2 us
    pallas_call x1, Pallas kernels, feed(): pl.pallas_call(feed_kernel, out_shape=(S((tokens, width), F32), S((2, hid...  58.9 us
    pallas_call x1, Pallas kernels, attend_back(): pl.pallas_call(attend_back_kernel, out_shape=(S((half, width), F32), S((s...  45.8 us
    pallas_call x1, Pallas kernels, attend(): pl.pallas_call(attend_kernel, out_shape=(S((half, width), BF16), S((half,...  39 us
    unnamed x17, local copies, waits for them, and re-layouts  11.7 us

profile of v2, /device:TPU:0, one launch (start us, length us, event | category | flops | bytes accessed | tf_op | source)
XLA Modules:
  0.0 340.2 jit_solution(18399093907863982838)
XLA Ops:
  0.6 0.0 copy-start.4
  0.7 0.7 stack.23.place
  1.4 2.9 copy.23.wqkv
  4.4 0.0 copy-done.4
  4.4 0.6 reshape.32.bff1
  4.9 0.0 copy-start.3
  4.9 68.2 %gather_weights.1 = (bf16[3,768,768]{2,1,0:T(8,128)(2,1)}, bf16[768,768]{1,0:T(8,128)(2,1)}, bf16[4,768,768]{2,1,0:T(8,128)(2,1)}, bf16[4,768,768]{2,1,0:T(8,128)(2,1)}, f32[4,8,768]{2,1,0:T(8,128)}) custom-call(f32[3,768,192]{2,1,0:T(8,128)} %copy.23.wqkv, f32[192,768]{1,0:T(8,128)} %wout.1, f32[768,768]{1,0:T(8,128)} %wff1.1, f32[768,768]{1,0:T(8,128)} %wff2.1, ...), custom_call_target="tpu_custom_call" | custom-call | tf_op jit(solution)/shard_map/gather_weights/pallas_call | solution.py:233
  73.2 0.0 copy-done.3
  73.2 0.6 reshape.31.seg_ref
  73.8 39.0 %attend.1 = (bf16[1024,768]{1,0:T(8,128)(2,1)}, bf16[1024,768]{1,0:T(8,128)(2,1)}, bf16[1024,768]{1,0:T(8,128)(2,1)}, bf16[1024,768]{1,0:T(8,128)(2,1)}, bf16[24...) custom-call(s32[5]{0:T(128)} %stack.23.place, ...), custom_call_target="tpu_custom_call" | custom-call | tf_op jit(solution)/shard_map/attend/pallas_call | solution.py:330
  112.8 58.9 %feed.1 = (f32[1024,768]{1,0:T(8,128)}, bf16[2,768,768]{2,1,0:T(8,128)(2,1)}, bf16[2,768,768]{2,1,0:T(8,128)(2,1)}, bf16[1024,768]{1,0:T(8,128)(2,1)}, f32[1024,...) custom-call(s32[5]{0:T(128)} %stack.23.place, bf16[1024,768]{1,0:T(8,128)(2,1)} %get-tuple-element.44.nq_ref, ...), custom_call_target="tpu_custom_call" | custom-call | tf_op jit(solution)/shard_map/feed/pallas_call | solution.py:485
  171.6 0.0 copy-start.1
  171.7 0.0 copy-start.2
  171.7 45.8 %attend_back.1 = (f32[1024,768]{1,0:T(8,128)}, bf16[384,768]{1,0:T(8,128)(2,1)}, bf16[3,384,768]{2,1,0:T(8,128)(2,1)}, f32[8,384]{1,0:T(8,128)}) custom-call(s32[5]{0:T(128)} %stack.23.place, f32[2048,768]{1,0:T(8,128)} %x_ref.3, bf16[1024,768]{1,0:T(8,128)(2,1)} %get-tuple-element.51.xq_ref, bf16[1024,768]{1,0:T(8,128)(2,1)} %get-tuple-element.52.q_ref, ...), custom_call_target="tpu_custom_call" | custom-call | tf_op jit(solution)/shard_map/attend_back/pallas_call | solution.py:618
  217.4 0.7 slice.38
  218.2 0.0 copy-done.1
  218.2 0.0 copy-done.2
  218.2 0.6 select_maximum_fusion.smalls
  218.8 100.5 %reduce_grads.1 = (bf16[2304,768]{1,0:T(8,128)(2,1)}, f32[16,768]{1,0:T(8,128)}, f32[2048,768]{1,0:T(8,128)}, f32[2048,768]{1,0:T(8,128)}) custom-call(bf16[2,768,768]{2,1,0:T(8,128)(2,1)} %get-tuple-element.49.g2, bf16[2,768,768]{2,1,0:T(8,128)(2,1)} %get-tuple-element.50.g1, bf16[384,768]{1,0:T(8,128)(2,1)} %get-tuple-element.60.go, ...), custom_call_target="tpu_custom_call" | custom-call | tf_op jit(solution)/shard_map/reduce_grads/pallas_call | solution.py:956
  319.3 0.7 slice.44
  320.0 0.7 slice.40
  320.8 0.7 constant_dynamic-slice_fusion
  321.4 0.0 copy-start
  321.4 4.3 %fusion = (f32[768,768]{1,0:T(8,128)}, f32[768,768]{1,0:T(8,128)}) fusion(bf16[2304,768]{1,0:T(8,128)(2,1)} %get-tuple-element.69), kind=kLoop, calls=%fused_computation.6 | loop fusion | bytes 9437184 | tf_op jit(solution)/shard_map/slice | solution.py:1009
  325.8 0.0 copy-done
  325.8 1.3 slice.49
  327.1 0.0 slice-start
  327.1 0.9 slice.50
  327.9 0.7 dynamic-slice.1
  328.6 1.3 dynamic-slice_reduce_fusion
  330.0 1.0 slice.47
  330.9 0.5 reduce_max.9
  331.5 0.0 slice-start.1
  331.5 6.1 %copy.27 = f32[2048,768]{1,0:T(8,128)} copy(f32[2048,768]{1,0:T(8,128)} %get-tuple-element.86) | data formatting | bytes 12582912
  337.5 0.0 slice-done
  337.5 0.0 slice-done.1
  337.5 2.7 copy.28
  (3 shorter events, 0.0 us)
Async XLA Ops:
  0.6 3.7 %copy-start.4 = (f32[768]{0:T(1024)S(1)}, f32[768]{0:T(1024)}, u32[]{:S(2)}) copy-start(f32[768]{0:T(1024)} %param.18) | copy-start | bytes 9220
  4.9 68.2 %copy-start.3 = (s32[4,512]{1,0:T(4,128)S(1)}, s32[4,512]{1,0:T(4,128)}, u32[]{:S(2)}) copy-start(s32[4,512]{1,0:T(4,128)} %param.13) | copy-start | bytes 24580
  171.6 46.5 %copy-start.1 = (f32[2,8,768]{2,1,0:T(8,128)S(1)}, f32[2,8,768]{2,1,0:T(8,128)}, u32[]{:S(2)}) copy-start(f32[2,8,768]{2,1,0:T(8,128)} %get-tuple-element.63) | copy-start | bytes 147460
  171.7 46.5 %copy-start.2 = (f32[8,768]{1,0:T(8,128)S(1)}, f32[8,768]{1,0:T(8,128)}, u32[]{:S(2)}) copy-start(f32[8,768]{1,0:T(8,128)} %get-tuple-element.62) | copy-start | bytes 73732
  321.4 4.3 %copy-start = (bf16[2304,768]{1,0:T(8,128)(2,1)S(1)}, bf16[2304,768]{1,0:T(8,128)(2,1)}, u32[]{:S(2)}) copy-start(bf16[2304,768]{1,0:T(8,128)(2,1)} %get-tuple-element.69) | copy-start | bytes 10616836
  327.1 10.4 %slice-start = ((s8[6291456]{0:T(1024)(128)(4,1)}), s8[2097152]{0:T(1024)(128)(4,1)S(1)}, s32[]{:S(2)}) async-start(s8[6291456]{0:T(1024)(128)(4,1)} %bitcast.11), calls=%async_computation | async-start | bytes 4194304
  331.5 6.1 %slice-start.1 = ((s8[6291456]{0:T(1024)(128)(4,1)}), s8[4194304]{0:T(1024)(128)(4,1)S(1)}, s32[]{:S(2)}) async-start(s8[6291456]{0:T(1024)(128)(4,1)} %bitcast.11), calls=%async_computation.1 | async-start | bytes 8388608
